TPU v7x, 32 devices: a whole 2x2x4 slice. The times are simulated.
32 devices in a mesh: dp: 8 (over z, x), tensor: 4 (over y, core).
Axes of the slice: x: 2, y: 2, z: 4, core: 2. Of those that a mesh axis runs over, the one named last changes fastest.
Arguments:
- layer_input: bfloat16 [16384, 768], P(('dp', 'tensor')), may hold values from -6 to 6
- out_cotangent: bfloat16 [16384, 768], P(('dp', 'tensor')), may hold values from -6 to 6
- qkv_weight: bfloat16 [3, 768, 768], P(None, None, 'tensor'), may hold values from -0.21875 to 0.21875
- qv_bias: bfloat16 [2, 768], P(None, 'tensor'), may hold values from -1 to 1
- out_weight: bfloat16 [768, 768], P('tensor'), may hold values from -0.875 to 0.875
- out_bias: bfloat16 [768], replicated, may hold values from -1 to 1
- norm1_gain: bfloat16 [768], replicated, may hold values from 0.5 to 1.5
- norm1_bias: bfloat16 [768], replicated, may hold values from -1 to 1
- up_weight: bfloat16 [768, 3072], P(None, 'tensor'), may hold values from -0.21875 to 0.21875
- up_bias: bfloat16 [3072], P('tensor'), may hold values from -1 to 1
- down_weight: bfloat16 [3072, 768], P('tensor'), may hold values from -0.15625 to 0.15625
- down_bias: bfloat16 [768], replicated, may hold values from -1 to 1
- norm2_gain: bfloat16 [768], replicated, may hold values from 0.5 to 1.5
- norm2_bias: bfloat16 [768], replicated, may hold values from -1 to 1
- cluster_perm: int32 [32, 12, 512], P('dp', 'tensor'), may hold values from 0 to 511, each once within a row
- segment_ids: int32 [32, 512], P('dp'), may hold values from 0 to 3, never falling along the last dimension, each value on 1 to 256 neighbouring positions
Outputs:
- layer_output: bfloat16 [16384, 768], P(('dp', 'tensor'))
- input_grad: bfloat16 [16384, 768], P(('dp', 'tensor'))
- qkv_weight_grad: float32 [3, 768, 768], P(None, None, 'tensor')
- qv_bias_grad: float32 [2, 768], P(None, 'tensor')
- out_weight_grad: float32 [768, 768], P('tensor')
- out_bias_grad: float32 [768], replicated
- norm1_gain_grad: float32 [768], replicated
- norm1_bias_grad: float32 [768], replicated
- up_weight_grad: float32 [768, 3072], P(None, 'tensor')
- up_bias_grad: float32 [3072], P('tensor')
- down_weight_grad: float32 [3072, 768], P('tensor')
- down_bias_grad: float32 [768], replicated
- norm2_gain_grad: float32 [768], replicated
- norm2_bias_grad: float32 [768], replicated
Inputs may be any that keep to these rules, and one draw needn't show every extreme that they name: `cluster_perm`: each row of a head lists every position of its packed row once. `segment_ids`: never falls along a packed row; each id covers 1 to 256 consecutive positions.
All inputs are finite; a program needn't handle non-finite values.
Results may differ from a plain program's by a relative error of at most 0.02.
Values may be sent and summed in bfloat16 or wider, within the bound.
No kernel may reach another device: no remote copies, remote signals or barrier semaphores. Data moves between devices by JAX's collectives and lax.ppermute only.
A program may use at most 128 MiB of HBM per device.

v0:
```python
import math

import jax
import jax.numpy as jnp
from jax import lax
from jax.experimental import pallas as pl
from jax.experimental.pallas import tpu as pltpu
from jax.sharding import PartitionSpec as P

HEAD_DIM = 64
CLUSTER = 128
NORM_EPS = 1e-12
MASKED = -1000000000.0
ROOT_HALF = 0.7071067811865476
INV_ROOT_TWO_PI = 0.3989422804014327
SCALE = 1.0 / math.sqrt(HEAD_DIM)
SLOT = 4 * HEAD_DIM
PAIR = 2 * HEAD_DIM
BLOCK = 128
VMEM_LIMIT = 30 * 1024 * 1024
EXTRA = 64
F32 = jnp.float32
BF16 = jnp.bfloat16


def mm(a, b):
    return jnp.dot(a, b, preferred_element_type=F32)


def mm_nt(a, b):
    return lax.dot_general(a, b, (((1,), (1,)), ((), ())), preferred_element_type=F32)


def mm_tn(a, b):
    return lax.dot_general(a, b, (((0,), (0,)), ((), ())), preferred_element_type=F32)


def call(body, outs, scratch, micros, *args, after=()):
    shapes = [jax.ShapeDtypeStruct(s, t) for s, t in outs]
    kept = len(args)

    def placed(a):
        flat = a.ndim == 1 and a.dtype == jnp.int32
        return pl.BlockSpec(memory_space=pltpu.SMEM if flat else pltpu.VMEM)

    def run(*refs):
        body(*refs[:kept], *refs[kept + len(after) :])

    return pl.pallas_call(
        run,
        out_shape=shapes,
        in_specs=[placed(a) for a in args] + [pl.BlockSpec(memory_space=pl.ANY)] * len(after),
        out_specs=[pl.BlockSpec(memory_space=pltpu.VMEM)] * len(outs),
        scratch_shapes=scratch,
        cost_estimate=pl.CostEstimate(flops=int(micros * 1e9), bytes_accessed=0, transcendentals=0),
        compiler_params=pltpu.CompilerParams(vmem_limit_bytes=VMEM_LIMIT),
    )(*args, *after)


def tie(value, *others):
    return lax.optimization_barrier((value, *others))[0]


def norm(values):
    center = values - jnp.mean(values, axis=-1, keepdims=True)
    inverse = lax.rsqrt(jnp.mean(center * center, axis=-1, keepdims=True) + NORM_EPS)
    return center * inverse, inverse


def norm_back(grad_in, normed, inverse, gain):
    scaled = grad_in * gain
    return inverse * (
        scaled
        - jnp.mean(scaled, axis=-1, keepdims=True)
        - normed * jnp.mean(scaled * normed, axis=-1, keepdims=True)
    )


def colsum(v):
    return jnp.sum(v, axis=0, keepdims=True)


def assemble(scratch, half_ref, relayed_ref, side):
    rows = half_ref.shape[0]
    here, there = half_ref[...], relayed_ref[...]
    scratch[0:rows, :] = jnp.where(side == 0, here, there)
    scratch[rows : 2 * rows, :] = jnp.where(side == 0, there, here)


def prepare(where_ref, qkv_ref, out_ref, perm_ref, vec_ref, packed_ref, half_ref, small_ref, lines_ref):
    width = qkv_ref.shape[1]
    turned = out_ref[...].astype(F32).T.astype(BF16)
    heads = qkv_ref.shape[2] // HEAD_DIM
    for h in range(heads):
        cut = slice(h * HEAD_DIM, (h + 1) * HEAD_DIM)
        packed_ref[:, h * SLOT : (h + 1) * SLOT] = jnp.concatenate(
            [qkv_ref[0, :, cut], qkv_ref[2, :, cut], qkv_ref[1, :, cut], turned[:, cut]], axis=1
        )
    half = width // 2
    half_ref[...] = jnp.where(where_ref[0] == 0, packed_ref[0:half, :], packed_ref[half:width, :])
    lines = vec_ref[...].astype(F32)
    lines_ref[...] = lines
    seqs = perm_ref.shape[0]
    for s in range(seqs):
        small_ref[s * heads : (s + 1) * heads, :] = perm_ref[s].astype(F32)
    own = heads * HEAD_DIM
    blank = jnp.zeros((1, 2 * HEAD_DIM), F32)
    bias = []
    for h in range(heads):
        bias += [lines[7:8, h * HEAD_DIM : (h + 1) * HEAD_DIM], lines[7:8, own + h * HEAD_DIM : own + (h + 1) * HEAD_DIM], blank]
    length = small_ref.shape[1]
    for row, line in ((seqs * heads, lines[6:7, :]), (seqs * heads + 2, jnp.concatenate(bias, axis=1))):
        small_ref[row : row + 1, :] = line[:, 0:length]
        rest = line.shape[1] - length
        small_ref[row + 1 : row + 2, :] = jnp.concatenate([line[:, length:], jnp.zeros((1, length - rest), F32)], axis=1)


def unpack(packed_ref, qkv_ref, out_ref, vec_ref):
    width = packed_ref.shape[1]
    heads = width // SLOT
    rows = qkv_ref.shape[1]

    def field(at):
        return jnp.concatenate(
            [packed_ref[0:rows, h * SLOT + at * HEAD_DIM : h * SLOT + (at + 1) * HEAD_DIM] for h in range(heads)], axis=1
        ).astype(F32)

    qkv_ref[0], qkv_ref[2], qkv_ref[1] = field(0), field(1), field(2)
    out_ref[...] = field(3).T
    vec_ref[...] = packed_ref[rows : rows + 16, :].astype(F32)


def put_orders(where_ref, packs, seg_ref, order_ref, turned_ref):
    heads = order_ref.shape[0] // 2 - 1
    order_ref[...] = jnp.zeros_like(order_ref)
    for group, pack in enumerate(packs):
        for h in range(heads):
            at = group * heads + h
            order_ref[at : at + 1, :] = pack[pl.ds(where_ref[1] * heads + h, 1), :]
    order_ref[2 * heads : 2 * heads + 1, :] = seg_ref[pl.ds(where_ref[1], 1), :].astype(F32)
    turned_ref[...] = order_ref[...].T


def put_tables(order_ref, turned_ref, count, place_ref, position_ref):
    length = order_ref.shape[1]
    lane = lax.broadcasted_iota(jnp.int32, (length, length), 1).astype(F32)
    sub = lax.broadcasted_iota(jnp.int32, (length, length), 0).astype(F32)
    for at in range(count):
        place_ref[at] = jnp.where(turned_ref[:, at : at + 1] == lane, 1.0, 0.0).astype(BF16)
        position_ref[at] = jnp.where(order_ref[at : at + 1, :] == sub, 1.0, 0.0).astype(BF16)


def put_out_columns(weights, columns_ref):
    heads = weights[0].shape[1] // SLOT
    for group, w_ref in enumerate(weights):
        for h in range(heads):
            at = group * heads + h
            columns_ref[:, at * PAIR : (at + 1) * PAIR] = w_ref[:, h * SLOT + PAIR : (h + 1) * SLOT]


def cuts(length):
    return [slice(c, c + CLUSTER) for c in range(0, length, CLUSTER)]


def attend(
    x_ref, weights, packs, order_ref, turned_ref, fields_ref, probs_ref, ctx_ref,
    place_ref, position_ref, raw_ref, scores_ref, columns_ref,
):
    length = x_ref.shape[0]
    heads = weights[0].shape[1] // SLOT
    count = 2 * heads
    lanes = lax.broadcasted_iota(jnp.int32, (length, SLOT), 1)
    bias_row = packs[0].shape[0] - 2
    for group, (w_ref, pack) in enumerate(zip(weights, packs)):
        bias = jnp.concatenate([pack[bias_row : bias_row + 1, :], pack[bias_row + 1 : bias_row + 2, :]], axis=1)
        for h in range(heads):
            fields = mm(x_ref[...], w_ref[:, h * SLOT : (h + 1) * SLOT]) + bias[:, h * SLOT : (h + 1) * SLOT]
            raw_ref[group * heads + h] = jnp.where(lanes < 3 * HEAD_DIM, fields, turned_ref[:, count : count + 1]).astype(BF16)
    put_tables(order_ref, turned_ref, count, place_ref, position_ref)
    order_low = order_ref[...].astype(BF16)
    seg_rows = []
    for at in range(count):
        fields_ref[at] = mm(place_ref[at], raw_ref[at]).astype(BF16)
        seg_rows.append(mm(order_low, position_ref[at])[count : count + 1, :])
    for at in range(count):
        for c, cut in enumerate(cuts(length)):
            seg_col = fields_ref[at, cut, SLOT - PAIR : SLOT].astype(F32)[:, PAIR - 1 : PAIR]
            scores = mm_nt(fields_ref[at, cut, 0:HEAD_DIM], fields_ref[at, cut, PAIR : PAIR + HEAD_DIM]) * SCALE
            scores_ref[at, cut, :] = jnp.where(seg_col == seg_rows[at][:, cut], scores, MASKED)
    for at in range(count):
        for cut in cuts(length):
            scores = scores_ref[at, cut, :]
            raised = jnp.exp(scores - jnp.max(scores, axis=-1, keepdims=True))
            probs_ref[at, cut, :] = (raised / jnp.sum(raised, axis=-1, keepdims=True)).astype(BF16)
    low_lanes = lax.broadcasted_iota(jnp.int32, (CLUSTER, PAIR), 1) < HEAD_DIM
    for at in range(count):
        for cut in cuts(length):
            mixed = mm(probs_ref[at, cut, :], fields_ref[at, cut, 0:PAIR])
            raw_ref[at, cut, 0:PAIR] = jnp.where(low_lanes, 0.0, mixed).astype(BF16)
    for at in range(count):
        ctx_ref[:, at * PAIR : (at + 1) * PAIR] = mm(position_ref[at], raw_ref[at, :, 0:PAIR]).astype(BF16)
    put_out_columns(weights, columns_ref)


def near_attention(
    where_ref, x_ref, w0_ref, w1_ref, pack0_ref, pack1_ref, seg_ref,
    fields_ref, probs_ref, ctx_ref, sum_ref, order_ref, turned_ref,
    place_ref, position_ref, raw_ref, scores_ref, columns_ref,
):
    packs = (pack0_ref, pack1_ref)
    put_orders(where_ref, packs, seg_ref, order_ref, turned_ref)
    attend(
        x_ref, (w0_ref, w1_ref), packs, order_ref, turned_ref, fields_ref, probs_ref, ctx_ref,
        place_ref, position_ref, raw_ref, scores_ref, columns_ref,
    )
    sum_ref[...] = mm_nt(ctx_ref[...], columns_ref[...])


def blocks(length):
    return [slice(r, r + BLOCK) for r in range(0, length, BLOCK)]


def far_attention(
    where_ref, x_ref, a2_ref, b2_ref, a3_ref, b3_ref, pack2_ref, pack3_ref, seg_ref, sum_ref, vec_ref,
    fields_ref, probs_ref, ctx_ref, order_ref, turned_ref, low_ref, normed_ref, inverse_ref,
    place_ref, position_ref, raw_ref, scores_ref, columns_ref, w2_ref, w3_ref, total_ref,
):
    packs = (pack2_ref, pack3_ref)
    assemble(w2_ref, a2_ref, b2_ref, where_ref[0])
    assemble(w3_ref, a3_ref, b3_ref, where_ref[0])
    put_orders(where_ref, packs, seg_ref, order_ref, turned_ref)
    attend(
        x_ref, (w2_ref, w3_ref), packs, order_ref, turned_ref, fields_ref, probs_ref, ctx_ref,
        place_ref, position_ref, raw_ref, scores_ref, columns_ref,
    )
    total_ref[...] = mm_nt(ctx_ref[...], columns_ref[...])
    for r in blocks(x_ref.shape[0]):
        normed, inverse = norm(x_ref[r, :].astype(F32) + sum_ref[r, :] + total_ref[r, :] + vec_ref[0:1, :])
        low_ref[r, :] = (normed * vec_ref[1:2, :] + vec_ref[2:3, :]).astype(BF16)
        normed_ref[r, :] = normed
        inverse_ref[r, :] = inverse


def up_bias(pack_ref, width):
    row = pack_ref.shape[0] - 4
    return jnp.concatenate([pack_ref[row : row + 1, :], pack_ref[row + 1 : row + 2, :]], axis=1)[:, 0:width]


def hidden_units(low_ref, up_ref, shift, hidden_ref, slope_ref):
    length = low_ref.shape[0]
    for r in blocks(length):
        v = mm(low_ref[r, :], up_ref[...]) + shift
        half = 0.5 + 0.5 * lax.erf(v * ROOT_HALF)
        hidden_ref[r, :] = (v * half).astype(BF16)
        slope_ref[r, :] = (half + v * jnp.exp(-0.5 * v * v) * INV_ROOT_TWO_PI).astype(BF16)


def near_forward(low_ref, u0_ref, u1_ref, d0_ref, d1_ref, pack0_ref, pack1_ref, hidden_ref, slope_ref, sum_ref):
    width = u0_ref.shape[1]
    hidden_units(low_ref, u0_ref, up_bias(pack0_ref, width), hidden_ref.at[0], slope_ref.at[0])
    hidden_units(low_ref, u1_ref, up_bias(pack1_ref, width), hidden_ref.at[1], slope_ref.at[1])
    for r in blocks(low_ref.shape[0]):
        sum_ref[r, :] = mm(hidden_ref[0, r, :], d0_ref[...]) + mm(hidden_ref[1, r, :], d1_ref[...])


def far_up(where_ref, low_ref, a2_ref, b2_ref, a3_ref, b3_ref, pack2_ref, pack3_ref, hidden_ref, slope_ref, u2_ref, u3_ref):
    width = a2_ref.shape[1]
    assemble(u2_ref, a2_ref, b2_ref, where_ref[0])
    assemble(u3_ref, a3_ref, b3_ref, where_ref[0])
    hidden_units(low_ref, u2_ref, up_bias(pack2_ref, width), hidden_ref.at[0], slope_ref.at[0])
    hidden_units(low_ref, u3_ref, up_bias(pack3_ref, width), hidden_ref.at[1], slope_ref.at[1])


def far_down(
    where_ref, hidden_ref, a2_ref, b2_ref, a3_ref, b3_ref, sum_ref, normed_a_ref, cot_ref, vec_ref,
    out_ref, grad_ref, grad_low_ref, sums_ref, d2_ref, d3_ref,
):
    assemble(d2_ref, a2_ref, b2_ref, where_ref[0])
    assemble(d3_ref, a3_ref, b3_ref, where_ref[0])
    sums_ref[...] = jnp.zeros_like(sums_ref)
    for r in blocks(hidden_ref.shape[1]):
        total = sum_ref[r, :] + mm(hidden_ref[0, r, :], d2_ref[...]) + mm(hidden_ref[1, r, :], d3_ref[...])
        middle = normed_a_ref[r, :] * vec_ref[1:2, :] + vec_ref[2:3, :]
        normed, inverse = norm(middle + total + vec_ref[3:4, :])
        out_ref[r, :] = (normed * vec_ref[4:5, :] + vec_ref[5:6, :]).astype(BF16)
        cot = cot_ref[r, :].astype(F32)
        grad = norm_back(cot, normed, inverse, vec_ref[4:5, :])
        grad_ref[r, :] = grad
        grad_low_ref[r, :] = grad.astype(BF16)
        sums_ref[0:1, :] += colsum(cot * normed)
        sums_ref[1:2, :] += colsum(cot)
        sums_ref[2:3, :] += colsum(grad)


def down_grads(far_ref, near_ref, grad_low_ref, g3_ref, g2_ref, g1_ref, g0_ref):
    g3_ref[...] = mm_tn(far_ref[1], grad_low_ref[...]).astype(BF16)
    g2_ref[...] = mm_tn(far_ref[0], grad_low_ref[...]).astype(BF16)
    g1_ref[...] = mm_tn(near_ref[1], grad_low_ref[...]).astype(BF16)
    g0_ref[...] = mm_tn(near_ref[0], grad_low_ref[...]).astype(BF16)


def up_grads(grad_low_ref, low_ref, slope_ref, down_ref, up_ref, pre_ref, out_ref, mid_ref, first, sums_ref, at):
    pre = (mm_nt(grad_low_ref[...], down_ref[...]) * slope_ref[...].astype(F32)).astype(BF16)
    pre_ref[...] = pre
    sums_ref[at : at + 1, :] = colsum(pre.astype(F32))
    out_ref[...] = mm_tn(low_ref[...], pre_ref[...]).astype(BF16)
    part = mm_nt(pre_ref[...], up_ref[...])
    mid_ref[...] = part if first else mid_ref[...] + part


def far_up_grads(
    where_ref, grad_low_ref, low_ref, slope_ref, d2a_ref, d2b_ref, d3a_ref, d3b_ref, u2a_ref, u2b_ref, u3a_ref, u3b_ref,
    g3_ref, g2_ref, mid_ref, shift_ref, d2_ref, d3_ref, u2_ref, u3_ref, pre2_ref, pre3_ref,
):
    side = where_ref[0]
    shift_ref[...] = jnp.zeros_like(shift_ref)
    assemble(d3_ref, d3a_ref, d3b_ref, side)
    assemble(u3_ref, u3a_ref, u3b_ref, side)
    assemble(d2_ref, d2a_ref, d2b_ref, side)
    assemble(u2_ref, u2a_ref, u2b_ref, side)
    up_grads(grad_low_ref, low_ref, slope_ref.at[1], d3_ref, u3_ref, pre3_ref, g3_ref, mid_ref, True, shift_ref, 1)
    up_grads(grad_low_ref, low_ref, slope_ref.at[0], d2_ref, u2_ref, pre2_ref, g2_ref, mid_ref, False, shift_ref, 0)


def near_up_grads(
    grad_low_ref, low_ref, slope_ref, d0_ref, d1_ref, u0_ref, u1_ref, far_mid_ref, grad_b_ref, normed_ref, inverse_ref,
    vec_ref, g1_ref, g0_ref, grad_ref, grad_out_ref, shift_ref, sums_ref, pre0_ref, pre1_ref, mid_ref,
):
    shift_ref[...] = jnp.zeros_like(shift_ref)
    sums_ref[...] = jnp.zeros_like(sums_ref)
    up_grads(grad_low_ref, low_ref, slope_ref.at[1], d1_ref, u1_ref, pre1_ref, g1_ref, mid_ref, True, shift_ref, 1)
    up_grads(grad_low_ref, low_ref, slope_ref.at[0], d0_ref, u0_ref, pre0_ref, g0_ref, mid_ref, False, shift_ref, 0)
    for r in blocks(low_ref.shape[0]):
        total = mid_ref[r, :] + far_mid_ref[r, :] + grad_b_ref[r, :]
        normed = normed_ref[r, :]
        grad = norm_back(total, normed, inverse_ref[r, :], vec_ref[1:2, :])
        grad_ref[r, :] = grad
        grad_out_ref[r, :] = grad.astype(BF16)
        sums_ref[0:1, :] += colsum(total * normed)
        sums_ref[1:2, :] += colsum(total)
        sums_ref[2:3, :] += colsum(grad)


def attend_back(
    x_ref, grad_out_ref, weights, order_ref, turned_ref, fields_ref, probs_ref, ctx_ref, outs,
    sums_b_ref, sums_a_ref, shift_ref, place_ref, position_ref, columns_ref, grads_ref, moved_ref, raw_ref, tok_ref, scores_ref, low_ref,
):
    length, width = x_ref.shape
    heads = weights[0].shape[1] // SLOT
    count = 2 * heads
    put_tables(order_ref, turned_ref, count, place_ref, position_ref)
    put_out_columns(weights, columns_ref)
    grads_ref[...] = mm(grad_out_ref[...], columns_ref[...]).astype(BF16)
    for at in range(count):
        moved_ref[at] = mm(place_ref[at], grads_ref[:, at * PAIR : (at + 1) * PAIR]).astype(BF16)
    low_lanes = lax.broadcasted_iota(jnp.int32, (CLUSTER, PAIR), 1) < HEAD_DIM
    no_low = jnp.zeros((CLUSTER, PAIR), BF16)
    for at in range(count):
        for cut in cuts(length):
            values = jnp.where(low_lanes, no_low, fields_ref[at, cut, 0:PAIR])
            scores_ref[at, cut, :] = mm_nt(moved_ref[at, cut, :], values)
    for at in range(count):
        for cut in cuts(length):
            grad_probs = scores_ref[at, cut, :]
            probs = probs_ref[at, cut, :].astype(F32)
            delta = jnp.sum(grad_probs * probs, axis=-1, keepdims=True)
            low_ref[at, cut, :] = (probs * (grad_probs - delta)).astype(BF16)
    for at in range(count):
        for cut in cuts(length):
            grad_queries = mm(low_ref[at, cut, :], fields_ref[at, cut, PAIR:SLOT]) * SCALE
            grad_values = mm_tn(probs_ref[at, cut, :], moved_ref[at, cut, :])
            raw_ref[at, cut, 0:PAIR] = jnp.where(low_lanes, grad_queries, grad_values).astype(BF16)
    for at in range(count):
        for cut in cuts(length):
            grad_keys = mm_tn(low_ref[at, cut, :], fields_ref[at, cut, 0:PAIR]) * SCALE
            raw_ref[at, cut, PAIR:SLOT] = jnp.where(low_lanes, grad_keys, 0.0).astype(BF16)
    for group, out_ref in reversed(list(enumerate(outs))):
        for h in range(heads):
            at = group * heads + h
            tok_ref[group, :, h * SLOT : (h + 1) * SLOT] = mm(position_ref[at], raw_ref[at]).astype(BF16)
        out_grad = mm_tn(grad_out_ref[...], ctx_ref[:, group * heads * PAIR : (group + 1) * heads * PAIR])
        grad = mm_tn(x_ref[...], tok_ref[group])
        for h in range(heads):
            out_ref[0:width, h * SLOT : h * SLOT + PAIR] = grad[:, h * SLOT : h * SLOT + PAIR].astype(BF16)
            out_ref[0:width, h * SLOT + PAIR : (h + 1) * SLOT] = (
                grad[:, h * SLOT + PAIR : (h + 1) * SLOT] + out_grad[:, h * PAIR : (h + 1) * PAIR]
            ).astype(BF16)
        fields = colsum(tok_ref[group].astype(F32))
        block = jnp.concatenate([sums_b_ref[0:3, :], sums_a_ref[0:3, :], shift_ref[group : group + 1, :], fields], axis=0)
        zero = jnp.zeros((EXTRA - 8, width), F32)
        out_ref[width:, :] = jnp.concatenate([block, zero], axis=0).astype(BF16)


def far_attention_grads(
    where_ref, x_ref, grad_out_ref, a2_ref, b2_ref, a3_ref, b3_ref, order_ref, turned_ref, fields_ref, probs_ref, ctx_ref,
    sums_b_ref, sums_a_ref, shift_ref, g3_ref, g2_ref, sum_ref,
    place_ref, position_ref, columns_ref, grads_ref, moved_ref, raw_ref, tok_ref, scores_ref, low_ref, w2_ref, w3_ref,
):
    assemble(w2_ref, a2_ref, b2_ref, where_ref[0])
    assemble(w3_ref, a3_ref, b3_ref, where_ref[0])
    attend_back(
        x_ref, grad_out_ref, (w2_ref, w3_ref), order_ref, turned_ref, fields_ref, probs_ref, ctx_ref, (g2_ref, g3_ref),
        sums_b_ref, sums_a_ref, shift_ref, place_ref, position_ref, columns_ref, grads_ref, moved_ref, raw_ref, tok_ref, scores_ref, low_ref,
    )
    sum_ref[...] = mm_nt(tok_ref[0], w2_ref[...]) + mm_nt(tok_ref[1], w3_ref[...])


def near_attention_grads(
    x_ref, grad_out_ref, w0_ref, w1_ref, order_ref, turned_ref, fields_ref, probs_ref, ctx_ref,
    sums_b_ref, sums_a_ref, shift_ref, sum_ref, grad_a_ref, g1_ref, g0_ref, in_ref,
    place_ref, position_ref, columns_ref, grads_ref, moved_ref, raw_ref, tok_ref, scores_ref, low_ref,
):
    attend_back(
        x_ref, grad_out_ref, (w0_ref, w1_ref), order_ref, turned_ref, fields_ref, probs_ref, ctx_ref, (g0_ref, g1_ref),
        sums_b_ref, sums_a_ref, shift_ref, place_ref, position_ref, columns_ref, grads_ref, moved_ref, raw_ref, tok_ref, scores_ref, low_ref,
    )
    in_ref[...] = (mm_nt(tok_ref[0], w0_ref[...]) + mm_nt(tok_ref[1], w1_ref[...]) + sum_ref[...] + grad_a_ref[...]).astype(BF16)


def solution(mesh):
    dp_size, tensor_size = mesh.shape["dp"], mesh.shape["tensor"]
    levels = dp_size.bit_length() - 1

    def swap(v, axis, bit):
        size = tensor_size if axis == "tensor" else dp_size
        return lax.ppermute(v, axis, [(i, i ^ (1 << bit)) for i in range(size)])

    def core_swap(v):
        return swap(v, "tensor", 0)

    def chip_swap(v):
        return swap(v, "tensor", 1)

    def add(a, b):
        return lax.reduce_precision(a.astype(F32) + b.astype(F32), 8, 7).astype(BF16)

    def on_device(
        layer_input, out_cotangent, qkv_weight, qv_bias, out_weight, out_bias, norm1_gain, norm1_bias,
        up_weight, up_bias, down_weight, down_bias, norm2_gain, norm2_bias, cluster_perm, segment_ids,
    ):
        length, width = layer_input.shape
        seqs, heads, _ = cluster_perm.shape
        units = up_weight.shape[1]
        mine = lax.axis_index("tensor")
        place = lax.axis_index("dp")
        side = place & 1
        half = width // 2

        where_arg = jnp.stack([side, mine]).astype(jnp.int32)
        count = 2 * heads
        lines = jnp.concatenate(
            [out_bias, norm1_gain, norm1_bias, down_bias, norm2_gain, norm2_bias, up_bias, qv_bias.reshape(-1),
             jnp.zeros((2 * width - units - 2 * heads * HEAD_DIM,), BF16)]
        ).reshape(8, width)
        square, half_t = ((width, width), BF16), ((half, width), BF16)
        vec_t = ((8, width), F32)
        small_t = ((seqs * heads + 4, length), F32)
        packed, packed_half, small, vecs = call(
            prepare, [square, half_t, small_t, vec_t], [], 3, where_arg, qkv_weight, out_weight, cluster_perm, lines
        )

        def own_half(m):
            return lax.dynamic_slice_in_dim(m, side * half, half, axis=0)

        def gather(m, m_half):
            first = chip_swap(m_half)
            second = swap(first, "dp", 0)
            return core_swap(m), (first, second, core_swap(first), core_swap(second))

        small_2, small_1 = chip_swap(small), core_swap(small)
        halves = [packed_half, own_half(up_weight), own_half(down_weight)]
        c_first, u_first, d_first = [chip_swap(m) for m in halves]
        c1, u1, d1 = core_swap(packed), core_swap(up_weight), core_swap(down_weight)

        def relay(first):
            second = swap(first, "dp", 0)
            return first, second, core_swap(first), core_swap(second)

        fields_t = ((count, length, SLOT), BF16)
        probs_t = ((count, length, CLUSTER), BF16)
        ctx_t = ((length, count * PAIR), BF16)
        orders_t = [((8, length), F32), ((length, 8), F32)]
        rows_f, rows_b = ((length, width), F32), ((length, width), BF16)
        pair_b = ((2, length, units), BF16)
        tall = ((width + EXTRA, heads * SLOT), BF16)
        mat, rows_s = pltpu.VMEM((width, width), BF16), pltpu.VMEM((length, width), BF16)
        tables = [pltpu.VMEM((count, length, length), BF16)] * 2
        columns = pltpu.VMEM((width, count * PAIR), BF16)
        raw = pltpu.VMEM((count, length, SLOT), BF16)
        scores = pltpu.VMEM((count, length, CLUSTER), F32)
        back = tables + [columns, rows_s, pltpu.VMEM((count, length, PAIR), BF16), raw, pltpu.VMEM((2, length, width), BF16)]
        back += [scores, pltpu.VMEM((count, length, CLUSTER), BF16)]

        near_fields, near_probs, near_ctx, attn_sum, *near_orders = call(
            near_attention, [fields_t, probs_t, ctx_t, rows_f, *orders_t], [*tables, raw, scores, columns], 8,
            where_arg, layer_input, packed, c1, small, small_1, segment_ids, after=(small_2,),
        )
        small_3 = core_swap(tie(small_2, attn_sum))
        c_far = relay(tie(c_first, attn_sum))
        u_far = relay(tie(u_first, attn_sum))
        far_fields, far_probs, far_ctx, *far_orders, low, normed_a, inverse_a = call(
            far_attention, [fields_t, probs_t, ctx_t, *orders_t, rows_b, rows_f, ((length, 1), F32)],
            [*tables, raw, scores, columns, mat, mat, pltpu.VMEM((length, width), F32)], 9,
            where_arg, layer_input, *c_far, small_2, small_3, segment_ids, attn_sum, vecs,
        )
        d_far = relay(tie(d_first, low))
        near_hidden, near_slope, ffn_sum = call(
            near_forward, [pair_b, pair_b, rows_f], [], 6, low, up_weight, u1, down_weight, d1, small, small_1
        )
        far_hidden, far_slope = call(
            far_up, [pair_b, pair_b], [mat, mat], 5, where_arg, low, *u_far, small_2, small_3
        )
        layer_output, grad_b, grad_b_low, sums_b = call(
            far_down, [rows_b, rows_f, rows_b, vec_t], [mat, mat], 5,
            where_arg, far_hidden, *d_far, ffn_sum, normed_a, out_cotangent, vecs,
        )
        dg3, dg2, dg1, dg0 = call(down_grads, [square] * 4, [], 2.8, far_hidden, near_hidden, grad_b_low)
        ds3, ds1 = core_swap(dg3), core_swap(dg1)
        ug3, ug2, grad_mid, far_ub = call(
            far_up_grads, [square, square, rows_f, vec_t], [mat] * 4 + [rows_s] * 2, 0.1,
            where_arg, grad_b_low, low, far_slope, *d_far, *u_far,
        )
        us3 = core_swap(ug3)
        down_cross = add(dg2, tie(ds3, grad_mid))
        ug1, ug0, grad_a, grad_a_low, near_ub, sums_a = call(
            near_up_grads, [square, square, rows_f, rows_b, vec_t, vec_t], [rows_s, rows_s, pltpu.VMEM((length, width), F32)], 0.1,
            grad_b_low, low, near_slope, down_weight, d1, up_weight, u1, grad_mid, grad_b, normed_a, inverse_a, vecs,
            after=(down_cross,),
        )
        us1 = core_swap(ug1)
        up_cross = add(ug2, tie(us3, grad_a_low))
        cg3, cg2, in_sum = call(
            far_attention_grads, [tall, tall, rows_f], back + [mat, mat], 0.1,
            where_arg, layer_input, grad_a_low, *c_far, *far_orders, far_fields, far_probs, far_ctx, sums_b, sums_a, far_ub,
            after=(up_cross,),
        )
        cs3 = core_swap(cg3)
        down_total = add(add(dg0, ds1), tie(chip_swap(down_cross), in_sum))
        packed_cross = add(cg2, cs3)
        cg1, cg0, input_grad = call(
            near_attention_grads, [tall, tall, rows_b], back, 0.1,
            layer_input, grad_a_low, packed, c1, *near_orders, near_fields, near_probs, near_ctx,
            sums_b, sums_a, near_ub, in_sum, grad_a, after=(down_total, packed_cross),
        )
        up_total = add(add(ug0, us1), tie(chip_swap(up_cross), input_grad))
        packed_total = add(add(cg0, core_swap(cg1)), chip_swap(packed_cross))

        def reduce(total):
            for level in range(levels):
                rows = total.shape[0] // 2
                bit = (place >> level) & 1
                send = lax.dynamic_slice_in_dim(total, (1 - bit) * rows, rows, axis=0)
                keep = lax.dynamic_slice_in_dim(total, bit * rows, rows, axis=0)
                total = add(keep, swap(send, "dp", level))
            for level in reversed(range(levels)):
                bit = (place >> level) & 1
                other = swap(total, "dp", level)
                total = jnp.where(
                    bit == 0, jnp.concatenate([total, other], axis=0), jnp.concatenate([other, total], axis=0)
                )
            return total

        down_grad = reduce(down_total).astype(F32)
        up_grad = reduce(up_total).astype(F32)
        packed_grad = reduce(packed_total)
        qkv_grad, out_grad, sums = call(
            unpack,
            [((3, width, heads * HEAD_DIM), F32), ((heads * HEAD_DIM, width), F32), ((16, width), F32)], [], 1,
            packed_grad,
        )
        field_sums = sums[7].reshape(heads, 4, HEAD_DIM)
        qv_grad = jnp.stack([field_sums[:, 0].reshape(-1), field_sums[:, 1].reshape(-1)])
        return (
            layer_output, input_grad, qkv_grad, qv_grad, out_grad, sums[5], sums[3], sums[4],
            up_grad, sums[6], down_grad, sums[2], sums[0], sums[1],
        )

    rows, split, copied = P(("dp", "tensor"), None), P(None, "tensor"), P()
    in_specs = (
        rows, rows, P(None, None, "tensor"), split, P("tensor", None), copied, copied, copied, split, P("tensor"),
        P("tensor", None), copied, copied, copied, P("dp", "tensor", None), P("dp", None),
    )
    out_specs = (
        rows, rows, P(None, None, "tensor"), split, P("tensor", None), copied, copied, copied, split, P("tensor"),
        P("tensor", None), copied, copied, copied,
    )
    return jax.shard_map(on_device, mesh=mesh, in_specs=in_specs, out_specs=out_specs, check_vma=False)
```

profile of v0, /device:TPU:0, one launch (start us, length us, event | category | flops | bytes accessed | tf_op | source)
XLA Modules:
  0.0 278.7 jit_solution(6370590616649088295)
XLA Ops:
  11.5 6.6 %shard_map.264 = (bf16[6,512,256]{2,1,0:T(8,128)(2,1)S(1)}, bf16[6,512,128]{2,1,0:T(8,128)(2,1)S(1)}, bf16[512,768]{1,0:T(8,128)(2,1)S(1)}, f32[512,768]{1,0:T(8...) custom-call(s32[2]{0:T(128)S(1)} %pad_add_fusion.refs_0_, bf16[512,768]{1,0:T(8,128)(2,1)S(1)} %copy-done, ...), custom_call_target="tpu_custom_call" | custom-call | flops 8000000000 | tf_op jit(solution)/shard_map/pallas_call | solution.py:49
  27.3 11.9 %collective-permute-done.4.refs_3_.refs_4_ = bf16[384,768]{1,0:T(8,128)(2,1)} collective-permute-done((bf16[384,768]{1,0:T(8,128)(2,1)}, bf16[384,768]{1,0:T(8,128)(2,1)}, u32[]{:S(2)}, u32[]{:S(2)}) %collective-permute-start.4) | collective-permute-done | bytes 589856 | tf_op jit(solution)/shard_map/ppermute | solution.py:426
  46.5 8.1 %shard_map.265 = (bf16[6,512,256]{2,1,0:T(8,128)(2,1)S(1)}, bf16[6,512,128]{2,1,0:T(8,128)(2,1)S(1)}, bf16[512,768]{1,0:T(8,128)(2,1)S(1)}, f32[8,512]{1,0:T(8,1...) custom-call(s32[2]{0:T(128)S(1)} %pad_add_fusion.refs_0_, ...), custom_call_target="tpu_custom_call" | custom-call | flops 8999999488 | tf_op jit(solution)/shard_map/pallas_call | solution.py:49
  59.7 12.5 %collective-permute-done.13.refs_3_.refs_5_ = bf16[384,768]{1,0:T(8,128)(2,1)S(1)} collective-permute-done((bf16[384,768]{1,0:T(8,128)(2,1)S(1)}, bf16[384,768]{1,0:T(8,128)(2,1)S(1)}, u32[]{:S(2)}, u32[]{:S(2)}) %collective-permute-start.13) | collective-permute-done | bytes 589856 | tf_op jit(solution)/shard_map/ppermute | solution.py:426
  74.9 3.2 %shard_map.267 = (bf16[2,512,768]{2,1,0:T(8,128)(2,1)S(1)}, bf16[2,512,768]{2,1,0:T(8,128)(2,1)S(1)}, f32[512,768]{1,0:T(8,128)S(1)}) custom-call(bf16[512,768]{1,0:T(8,128)(2,1)S(1)} %get-tuple-element.79.refs_1_.refs_0_.refs_2_, bf16[768,768]{1,0:T(8,128)(2,1)S(1)} %copy-done.3, bf16[768,768]{1,0:T(8,128)(2,1)S(1)} %collective-permute-done.16.refs_2_.refs_6_, ...), custom_call_target="tpu_custom_call" | custom-call | flops 6000000000 | tf_op jit(solution)/shard_map/pallas_call | solution.py:49
  78.2 3.8 %shard_map.268 = (bf16[512,768]{1,0:T(8,128)(2,1)}, f32[512,768]{1,0:T(8,128)S(1)}, bf16[512,768]{1,0:T(8,128)(2,1)S(1)}, f32[8,768]{1,0:T(8,128)S(1)}) custom-call(s32[2]{0:T(128)S(1)} %pad_add_fusion.refs_0_, bf16[2,512,768]{2,1,0:T(8,128)(2,1)S(1)} %get-tuple-element.81.refs_1_.refs_0_, bf16[384,768]{1,0:T(8,128)(2,1)S(1)} %collective-permute-done.12.refs_2_.refs_4_, ...), custom_call_target="tpu_custom_call" | custom-call | flops 5000000000 | tf_op jit(solution)/shard_map/pallas_call | solution.py:49
  83.4 3.2 %shard_map.270 = (bf16[768,768]{1,0:T(8,128)(2,1)S(1)}, bf16[768,768]{1,0:T(8,128)(2,1)S(1)}, bf16[768,768]{1,0:T(8,128)(2,1)}, bf16[768,768]{1,0:T(8,128)(2,1)S(1)}) custom-call(bf16[2,512,768]{2,1,0:T(8,128)(2,1)S(1)} %copy-done.45, bf16[2,512,768]{2,1,0:T(8,128)(2,1)S(1)} %get-tuple-element.92.refs_1_, ...), custom_call_target="tpu_custom_call" | custom-call | flops 2800000000 | tf_op jit(solution)/shard_map/pallas_call | solution.py:49
  87.7 5.2 %shard_map.269 = (bf16[768,768]{1,0:T(8,128)(2,1)S(1)}, bf16[768,768]{1,0:T(8,128)(2,1)S(1)}, f32[512,768]{1,0:T(8,128)S(1)}, f32[8,768]{1,0:T(8,128)S(1)}) custom-call(s32[2]{0:T(128)S(1)} %pad_add_fusion.refs_0_, bf16[512,768]{1,0:T(8,128)(2,1)S(1)} %get-tuple-element.86.refs_1_.refs_2_.refs_0_, ...), custom_call_target="tpu_custom_call" | custom-call | flops 100000000 | tf_op jit(solution)/shard_map/pallas_call | solution.py:49
  95.3 6.1 %shard_map.271 = (bf16[768,768]{1,0:T(8,128)(2,1)}, bf16[768,768]{1,0:T(8,128)(2,1)S(1)}, f32[512,768]{1,0:T(8,128)S(1)}, bf16[512,768]{1,0:T(8,128)(2,1)S(1)}, ...) custom-call(bf16[512,768]{1,0:T(8,128)(2,1)S(1)} %get-tuple-element.86.refs_1_.refs_2_.refs_0_, ...), custom_call_target="tpu_custom_call" | custom-call | flops 100000000 | tf_op jit(solution)/shard_map/pallas_call | solution.py:49
  104.1 10.2 %shard_map.272 = (bf16[832,768]{1,0:T(8,128)(2,1)}, bf16[832,768]{1,0:T(8,128)(2,1)S(1)}, f32[512,768]{1,0:T(8,128)S(1)}) custom-call(s32[2]{0:T(128)S(1)} %copy-done.36, bf16[512,768]{1,0:T(8,128)(2,1)S(1)} %copy-done, bf16[512,768]{1,0:T(8,128)(2,1)S(1)} %get-tuple-element.96.refs_2_.refs_1_, bf16[384,768]{1,0:T(8,128)(2,1)} %collective-permute-done.refs_2_.refs_3_, ...), custom_call_target="tpu_custom_call" | custom-call | flops 100000000 | tf_op jit(solution)/shard_map/pallas_call | solution.py:49
  116.9 5.9 %collective-permute-done.21 = bf16[768,768]{1,0:T(8,128)(2,1)} collective-permute-done((bf16[768,768]{1,0:T(8,128)(2,1)S(1)}, bf16[768,768]{1,0:T(8,128)(2,1)}, u32[]{:S(2)}, u32[]{:S(2)}) %collective-permute-start.21) | collective-permute-done | bytes 1179680 | tf_op jit(solution)/shard_map/ppermute | solution.py:426
  131.5 8.4 %shard_map.273 = (bf16[832,768]{1,0:T(8,128)(2,1)}, bf16[832,768]{1,0:T(8,128)(2,1)S(1)}, bf16[512,768]{1,0:T(8,128)(2,1)}) custom-call(bf16[512,768]{1,0:T(8,128)(2,1)S(1)} %copy-done, bf16[512,768]{1,0:T(8,128)(2,1)S(1)} %copy-done.2, bf16[768,768]{1,0:T(8,128)(2,1)S(1)} %copy-done.17, bf16[768,768]{1,0:T(8,128)(2,1)S(1)} %copy-done.19, ...), custom_call_target="tpu_custom_call" | custom-call | flops 100000000 | tf_op jit(solution)/shard_map/pallas_call | solution.py:49
  140.0 8.2 %collective-permute-done.32 = bf16[768,768]{1,0:T(8,128)(2,1)} collective-permute-done((bf16[768,768]{1,0:T(8,128)(2,1)}, bf16[768,768]{1,0:T(8,128)(2,1)}, u32[]{:S(2)}, u32[]{:S(2)}) %collective-permute-start.32) | collective-permute-done | bytes 1179680 | tf_op jit(solution)/shard_map/ppermute | solution.py:426
  155.9 9.1 %collective-permute-done.33 = bf16[384,768]{1,0:T(8,128)(2,1)} collective-permute-done((bf16[384,768]{1,0:T(8,128)(2,1)S(1)}, bf16[384,768]{1,0:T(8,128)(2,1)}, u32[]{:S(2)}, u32[]{:S(2)}) %collective-permute-start.33) | collective-permute-done | bytes 589856 | tf_op jit(solution)/shard_map/ppermute | solution.py:426
  166.2 8.4 %collective-permute-done.24 = bf16[832,768]{1,0:T(8,128)(2,1)} collective-permute-done((bf16[832,768]{1,0:T(8,128)(2,1)S(1)}, bf16[832,768]{1,0:T(8,128)(2,1)}, u32[]{:S(2)}, u32[]{:S(2)}) %collective-permute-start.24) | collective-permute-done | bytes 1277984 | tf_op jit(solution)/shard_map/ppermute | solution.py:426
  183.0 6.7 %collective-permute-done.34 = bf16[192,768]{1,0:T(8,128)(2,1)S(1)} collective-permute-done((bf16[192,768]{1,0:T(8,128)(2,1)S(1)}, bf16[192,768]{1,0:T(8,128)(2,1)S(1)}, u32[]{:S(2)}, u32[]{:S(2)}) %collective-permute-start.34) | collective-permute-done | bytes 294944 | tf_op jit(solution)/shard_map/ppermute | solution.py:426
  197.7 8.7 %collective-permute-done.26 = bf16[208,768]{1,0:T(8,128)(2,1)S(1)} collective-permute-done((bf16[208,768]{1,0:T(8,128)(2,1)S(1)}, bf16[208,768]{1,0:T(8,128)(2,1)S(1)}, u32[]{:S(2)}, u32[]{:S(2)}) %collective-permute-start.26) | collective-permute-done | bytes 319520 | tf_op jit(solution)/shard_map/ppermute | solution.py:426
  209.6 10.4 %collective-permute-done.27 = bf16[104,768]{1,0:T(8,128)(2,1)S(1)} collective-permute-done((bf16[104,768]{1,0:T(8,128)(2,1)S(1)}, bf16[104,768]{1,0:T(8,128)(2,1)S(1)}, u32[]{:S(2)}, u32[]{:S(2)}) %collective-permute-start.27) | collective-permute-done | bytes 159776 | tf_op jit(solution)/shard_map/ppermute | solution.py:426
  222.0 4.5 %collective-permute-done.36 = bf16[96,768]{1,0:T(8,128)(2,1)S(1)} collective-permute-done((bf16[96,768]{1,0:T(8,128)(2,1)S(1)}, bf16[96,768]{1,0:T(8,128)(2,1)S(1)}, u32[]{:S(2)}, u32[]{:S(2)}) %collective-permute-start.36) | collective-permute-done | bytes 147488 | tf_op jit(solution)/shard_map/ppermute | solution.py:426
  229.8 4.2 %collective-permute-done.43 = bf16[192,768]{1,0:T(8,128)(2,1)S(1)} collective-permute-done((bf16[192,768]{1,0:T(8,128)(2,1)S(1)}, bf16[192,768]{1,0:T(8,128)(2,1)S(1)}, u32[]{:S(2)}, u32[]{:S(2)}) %collective-permute-start.43) | collective-permute-done | bytes 294944 | tf_op jit(solution)/shard_map/ppermute | solution.py:426
  235.8 4.6 %collective-permute-done.37 = bf16[192,768]{1,0:T(8,128)(2,1)S(1)} collective-permute-done((bf16[192,768]{1,0:T(8,128)(2,1)S(1)}, bf16[192,768]{1,0:T(8,128)(2,1)S(1)}, u32[]{:S(2)}, u32[]{:S(2)}) %collective-permute-start.37) | collective-permute-done | bytes 294944 | tf_op jit(solution)/shard_map/ppermute | solution.py:426
  242.1 3.8 %collective-permute-done.29 = bf16[208,768]{1,0:T(8,128)(2,1)S(1)} collective-permute-done((bf16[208,768]{1,0:T(8,128)(2,1)S(1)}, bf16[208,768]{1,0:T(8,128)(2,1)S(1)}, u32[]{:S(2)}, u32[]{:S(2)}) %collective-permute-start.29) | collective-permute-done | bytes 319520 | tf_op jit(solution)/shard_map/ppermute | solution.py:426
  252.2 11.1 %collective-permute-done.38 = bf16[384,768]{1,0:T(8,128)(2,1)} collective-permute-done((bf16[384,768]{1,0:T(8,128)(2,1)S(1)}, bf16[384,768]{1,0:T(8,128)(2,1)}, u32[]{:S(2)}, u32[]{:S(2)}) %collective-permute-start.38) | collective-permute-done | bytes 589856 | tf_op jit(solution)/shard_map/ppermute | solution.py:426
  266.2 7.2 %collective-permute-done.30 = bf16[416,768]{1,0:T(8,128)(2,1)S(1)} collective-permute-done((bf16[416,768]{1,0:T(8,128)(2,1)S(1)}, bf16[416,768]{1,0:T(8,128)(2,1)S(1)}, u32[]{:S(2)}, u32[]{:S(2)}) %collective-permute-start.30) | collective-permute-done | bytes 639008 | tf_op jit(solution)/shard_map/ppermute | solution.py:426
  (254 shorter events, 104.6 us)
Async XLA Ops:
  9.6 15.1 %collective-permute-start = (bf16[384,768]{1,0:T(8,128)(2,1)S(1)}, bf16[384,768]{1,0:T(8,128)(2,1)}, u32[]{:S(2)}, u32[]{:S(2)}) collective-permute-start(bf16[384,768]{1,0:T(8,128)(2,1)S(1)} %get-tuple-element.72), channel_id=1, source_target_pairs={{0,2},{1,3},{2,0},{3,1},{4,6},{5,7},{6,4},{7,5},{8,10},{9,11},{10,... | collective-permute-start | bytes 1769480 | tf_op jit(solution)/shard_map/ppermute | solution.py:426
  27.3 16.3 %collective-permute-start.5 = (bf16[384,768]{1,0:T(8,128)(2,1)}, bf16[384,768]{1,0:T(8,128)(2,1)S(1)}, u32[]{:S(2)}, u32[]{:S(2)}) collective-permute-start(bf16[384,768]{1,0:T(8,128)(2,1)} %collective-permute-done.refs_2_.refs_3_), channel_id=1, source_target_pairs={{0,1},{1,0},{2,3},{3,2},{4,5},{5,4},{6,7},{7,6},{8,9},{9,8},{10,11... | collective-permute-start | bytes 1769480 | tf_op jit(solution)/shard_map/ppermute | solution.py:426
  39.2 35.7 %collective-permute-start.16 = (bf16[768,768]{1,0:T(8,128)(2,1)S(1)}, bf16[768,768]{1,0:T(8,128)(2,1)S(1)}, u32[]{:S(2)}, u32[]{:S(2)}) collective-permute-start(bf16[768,768]{1,0:T(8,128)(2,1)S(1)} %copy-done.3), channel_id=1, source_target_pairs={{0,1},{1,0},{2,3},{3,2},{4,5},{5,4},{6,7},{7,6},{8,9},{9,8},{10,11... | collective-permute-start | bytes 3538952 | tf_op jit(solution)/shard_map/ppermute | solution.py:426
  40.2 34.7 %collective-permute-start.17 = (bf16[768,768]{1,0:T(8,128)(2,1)S(1)}, bf16[768,768]{1,0:T(8,128)(2,1)S(1)}, u32[]{:S(2)}, u32[]{:S(2)}) collective-permute-start(bf16[768,768]{1,0:T(8,128)(2,1)S(1)} %copy-done.5), channel_id=1, source_target_pairs={{0,1},{1,0},{2,3},{3,2},{4,5},{5,4},{6,7},{7,6},{8,9},{9,8},{10,11... | collective-permute-start | bytes 3538952 | tf_op jit(solution)/shard_map/ppermute | solution.py:426
  42.3 15.4 %collective-permute-start.12 = (bf16[384,768]{1,0:T(8,128)(2,1)S(1)}, bf16[384,768]{1,0:T(8,128)(2,1)S(1)}, u32[]{:S(2)}, u32[]{:S(2)}) collective-permute-start(bf16[384,768]{1,0:T(8,128)(2,1)S(1)} %constant_dynamic-slice_fusion.9), channel_id=1, source_target_pairs={{0,2},{1,3},{2,0},{3,1},{4,6},{5,7},{6,4},{7,5},{8,10},{9,11},{10,... | collective-permute-start | bytes 1769480 | tf_op jit(solution)/shard_map/ppermute | solution.py:426
  43.6 15.6 %collective-permute-start.9 = (bf16[384,768]{1,0:T(8,128)(2,1)S(1)}, bf16[384,768]{1,0:T(8,128)(2,1)S(1)}, u32[]{:S(2)}, u32[]{:S(2)}) collective-permute-start(bf16[384,768]{1,0:T(8,128)(2,1)S(1)} %collective-permute-done.8.refs_2_.refs_8_), channel_id=1, source_target_pairs={{0,4},{4,0},{8,12},{12,8},{16,20},{20,16},{24,28},{28,24},{1,5},{5... | collective-permute-start | bytes 1769480 | tf_op jit(solution)/shard_map/ppermute | solution.py:426
  57.7 14.5 %collective-permute-start.13 = (bf16[384,768]{1,0:T(8,128)(2,1)S(1)}, bf16[384,768]{1,0:T(8,128)(2,1)S(1)}, u32[]{:S(2)}, u32[]{:S(2)}) collective-permute-start(bf16[384,768]{1,0:T(8,128)(2,1)S(1)} %collective-permute-done.12.refs_2_.refs_4_), channel_id=1, source_target_pairs={{0,4},{4,0},{8,12},{12,8},{16,20},{20,16},{24,28},{28,24},{1,5},{5... | collective-permute-start | bytes 1769480 | tf_op jit(solution)/shard_map/ppermute | solution.py:426
  59.2 18.9 %collective-permute-start.14 = (bf16[384,768]{1,0:T(8,128)(2,1)S(1)}, bf16[384,768]{1,0:T(8,128)(2,1)S(1)}, u32[]{:S(2)}, u32[]{:S(2)}) collective-permute-start(bf16[384,768]{1,0:T(8,128)(2,1)S(1)} %collective-permute-done.12.refs_2_.refs_4_), channel_id=1, source_target_pairs={{0,1},{1,0},{2,3},{3,2},{4,5},{5,4},{6,7},{7,6},{8,9},{9,8},{10,11... | collective-permute-start | bytes 1769480 | tf_op jit(solution)/shard_map/ppermute | solution.py:426
  93.9 29.0 %collective-permute-start.21 = (bf16[768,768]{1,0:T(8,128)(2,1)S(1)}, bf16[768,768]{1,0:T(8,128)(2,1)}, u32[]{:S(2)}, u32[]{:S(2)}) collective-permute-start(bf16[768,768]{1,0:T(8,128)(2,1)S(1)} %reduce-precision_convert_fusion.8.refs_12_), channel_id=1, source_target_pairs={{0,2},{1,3},{2,0},{3,1},{4,6},{5,7},{6,4},{7,5},{8,10},{9,11},{10,... | collective-permute-start | bytes 3538952 | tf_op jit(solution)/shard_map/ppermute | solution.py:426
  95.2 27.6 %collective-permute-start.20 = (bf16[768,768]{1,0:T(8,128)(2,1)}, bf16[768,768]{1,0:T(8,128)(2,1)}, u32[]{:S(2)}, u32[]{:S(2)}) collective-permute-start(bf16[768,768]{1,0:T(8,128)(2,1)} %get-tuple-element.117), channel_id=1, source_target_pairs={{0,1},{1,0},{2,3},{3,2},{4,5},{5,4},{6,7},{7,6},{8,9},{9,8},{10,11... | collective-permute-start | bytes 3538952 | tf_op jit(solution)/shard_map/ppermute | solution.py:426
  116.0 32.2 %collective-permute-start.32 = (bf16[768,768]{1,0:T(8,128)(2,1)}, bf16[768,768]{1,0:T(8,128)(2,1)}, u32[]{:S(2)}, u32[]{:S(2)}) collective-permute-start(bf16[768,768]{1,0:T(8,128)(2,1)} %reduce-precision_convert_fusion.7.refs_15_), channel_id=1, source_target_pairs={{0,2},{1,3},{2,0},{3,1},{4,6},{5,7},{6,4},{7,5},{8,10},{9,11},{10,... | collective-permute-start | bytes 3538952 | tf_op jit(solution)/shard_map/ppermute | solution.py:426
  116.7 31.4 %collective-permute-start.31 = (bf16[768,768]{1,0:T(8,128)(2,1)}, bf16[768,768]{1,0:T(8,128)(2,1)}, u32[]{:S(2)}, u32[]{:S(2)}) collective-permute-start(bf16[768,768]{1,0:T(8,128)(2,1)} %get-tuple-element.128), channel_id=1, source_target_pairs={{0,1},{1,0},{2,3},{3,2},{4,5},{5,4},{6,7},{7,6},{8,9},{9,8},{10,11... | collective-permute-start | bytes 3538952 | tf_op jit(solution)/shard_map/ppermute | solution.py:426
  126.4 26.5 %collective-permute-start.39 = (bf16[384,768]{1,0:T(8,128)(2,1)}, bf16[384,768]{1,0:T(8,128)(2,1)}, u32[]{:S(2)}, u32[]{:S(2)}) collective-permute-start(bf16[384,768]{1,0:T(8,128)(2,1)} %constant_dynamic-slice_fusion.2), channel_id=1, source_target_pairs={{0,4},{4,0},{8,12},{12,8},{16,20},{20,16},{24,28},{28,24},{1,5},{5... | collective-permute-start | bytes 1769480 | tf_op jit(solution)/shard_map/ppermute | solution.py:426
  130.1 44.5 %collective-permute-start.24 = (bf16[832,768]{1,0:T(8,128)(2,1)S(1)}, bf16[832,768]{1,0:T(8,128)(2,1)}, u32[]{:S(2)}, u32[]{:S(2)}) collective-permute-start(bf16[832,768]{1,0:T(8,128)(2,1)S(1)} %reduce-precision_convert_fusion.2.refs_15_), channel_id=1, source_target_pairs={{0,2},{1,3},{2,0},{3,1},{4,6},{5,7},{6,4},{7,5},{8,10},{9,11},{10,... | collective-permute-start | bytes 3833864 | tf_op jit(solution)/shard_map/ppermute | solution.py:426
  140.0 34.7 %collective-permute-start.23 = (bf16[832,768]{1,0:T(8,128)(2,1)}, bf16[832,768]{1,0:T(8,128)(2,1)}, u32[]{:S(2)}, u32[]{:S(2)}) collective-permute-start(bf16[832,768]{1,0:T(8,128)(2,1)} %get-tuple-element.123), channel_id=1, source_target_pairs={{0,1},{1,0},{2,3},{3,2},{4,5},{5,4},{6,7},{7,6},{8,9},{9,8},{10,11... | collective-permute-start | bytes 3833864 | tf_op jit(solution)/shard_map/ppermute | solution.py:426
  154.2 26.0 %collective-permute-start.40 = (bf16[192,768]{1,0:T(8,128)(2,1)S(1)}, bf16[192,768]{1,0:T(8,128)(2,1)S(1)}, u32[]{:S(2)}, u32[]{:S(2)}) collective-permute-start(bf16[192,768]{1,0:T(8,128)(2,1)S(1)} %constant_dynamic-slice_fusion.1), channel_id=1, source_target_pairs={{0,8},{4,12},{8,0},{12,4},{16,24},{20,28},{24,16},{28,20},{1,9},{5... | collective-permute-start | bytes 884744 | tf_op jit(solution)/shard_map/ppermute | solution.py:426
  177.0 15.6 %collective-permute-start.25 = (bf16[416,768]{1,0:T(8,128)(2,1)S(1)}, bf16[416,768]{1,0:T(8,128)(2,1)S(1)}, u32[]{:S(2)}, u32[]{:S(2)}) collective-permute-start(bf16[416,768]{1,0:T(8,128)(2,1)S(1)} %constant_dynamic-slice_fusion.8), channel_id=1, source_target_pairs={{0,4},{4,0},{8,12},{12,8},{16,20},{20,16},{24,28},{28,24},{1,5},{5... | collective-permute-start | bytes 1916936 | tf_op jit(solution)/shard_map/ppermute | solution.py:426
  180.3 16.7 %collective-permute-start.41 = (bf16[96,768]{1,0:T(8,128)(2,1)S(1)}, bf16[96,768]{1,0:T(8,128)(2,1)S(1)}, u32[]{:S(2)}, u32[]{:S(2)}) collective-permute-start(bf16[96,768]{1,0:T(8,128)(2,1)S(1)} %constant_dynamic-slice_fusion), channel_id=1, source_target_pairs={{0,16},{4,20},{8,24},{12,28},{16,0},{20,4},{24,8},{28,12},{1,17},{... | collective-permute-start | bytes 442376 | tf_op jit(solution)/shard_map/ppermute | solution.py:426
  197.1 23.0 %collective-permute-start.42 = (bf16[96,768]{1,0:T(8,128)(2,1)S(1)}, bf16[96,768]{1,0:T(8,128)(2,1)S(1)}, u32[]{:S(2)}, u32[]{:S(2)}) collective-permute-start(bf16[96,768]{1,0:T(8,128)(2,1)S(1)} %reduce-precision_convert_fusion.16), channel_id=1, source_target_pairs={{0,16},{4,20},{8,24},{12,28},{16,0},{20,4},{24,8},{28,12},{1,17},{... | collective-permute-start | bytes 442376 | tf_op jit(solution)/shard_map/ppermute | solution.py:426
  208.0 18.6 %collective-permute-start.36 = (bf16[96,768]{1,0:T(8,128)(2,1)S(1)}, bf16[96,768]{1,0:T(8,128)(2,1)S(1)}, u32[]{:S(2)}, u32[]{:S(2)}) collective-permute-start(bf16[96,768]{1,0:T(8,128)(2,1)S(1)} %reduce-precision_convert_fusion.17), channel_id=1, source_target_pairs={{0,16},{4,20},{8,24},{12,28},{16,0},{20,4},{24,8},{28,12},{1,17},{... | collective-permute-start | bytes 442376 | tf_op jit(solution)/shard_map/ppermute | solution.py:426
  229.7 16.2 %collective-permute-start.29 = (bf16[208,768]{1,0:T(8,128)(2,1)S(1)}, bf16[208,768]{1,0:T(8,128)(2,1)S(1)}, u32[]{:S(2)}, u32[]{:S(2)}) collective-permute-start(bf16[208,768]{1,0:T(8,128)(2,1)S(1)} %maximum_select_fusion.6), channel_id=1, source_target_pairs={{0,8},{4,12},{8,0},{12,4},{16,24},{20,28},{24,16},{28,20},{1,9},{5... | collective-permute-start | bytes 958472 | tf_op jit(solution)/shard_map/ppermute | solution.py:426
  234.2 16.3 %collective-permute-start.44 = (bf16[384,768]{1,0:T(8,128)(2,1)S(1)}, bf16[384,768]{1,0:T(8,128)(2,1)S(1)}, u32[]{:S(2)}, u32[]{:S(2)}) collective-permute-start(bf16[384,768]{1,0:T(8,128)(2,1)S(1)} %maximum_select_fusion.5), channel_id=1, source_target_pairs={{0,4},{4,0},{8,12},{12,8},{16,20},{20,16},{24,28},{28,24},{1,5},{5... | collective-permute-start | bytes 1769480 | tf_op jit(solution)/shard_map/ppermute | solution.py:426
  240.5 22.8 %collective-permute-start.38 = (bf16[384,768]{1,0:T(8,128)(2,1)S(1)}, bf16[384,768]{1,0:T(8,128)(2,1)}, u32[]{:S(2)}, u32[]{:S(2)}) collective-permute-start(bf16[384,768]{1,0:T(8,128)(2,1)S(1)} %maximum_select_fusion.4), channel_id=1, source_target_pairs={{0,4},{4,0},{8,12},{12,8},{16,20},{20,16},{24,28},{28,24},{1,5},{5... | collective-permute-start | bytes 1769480 | tf_op jit(solution)/shard_map/ppermute | solution.py:426
  246.1 27.2 %collective-permute-start.30 = (bf16[416,768]{1,0:T(8,128)(2,1)S(1)}, bf16[416,768]{1,0:T(8,128)(2,1)S(1)}, u32[]{:S(2)}, u32[]{:S(2)}) collective-permute-start(bf16[416,768]{1,0:T(8,128)(2,1)S(1)} %maximum_select_fusion.3), channel_id=1, source_target_pairs={{0,4},{4,0},{8,12},{12,8},{16,20},{20,16},{24,28},{28,24},{1,5},{5... | collective-permute-start | bytes 1916936 | tf_op jit(solution)/shard_map/ppermute | solution.py:426
  (80 other events, 641.9 us)
where the time goes:
time: 282 us; the launch traced here: 279 us
  waiting for transfers between devices  134 us (48%)
  Pallas kernels  59.9 us (21%)
  starting transfers between devices  41.8 us (15%)
  other arithmetic  20.7 us (7%)
  local copies, waits for them, and re-layouts  20.5 us (7%)
    ppermute x45, waiting for transfers between devices, swap(): return lax.ppermute(v, axis, [(i, i ^ 1 << bit) for i in range(size)])  134 us
    pallas_call x12, Pallas kernels, call(): pl.pallas_call(run, out_shape=shapes, in_specs=[placed(a) for a in args]...  59.9 us
    ppermute x45, starting transfers between devices, swap(): return lax.ppermute(v, axis, [(i, i ^ 1 << bit) for i in range(size)])  41.8 us
    unnamed x129, local copies, waits for them, and re-layouts  17.6 us
    convert_element_type x15, other arithmetic, add(): lax.reduce_precision(a.astype(F32) + b.astype(F32), 8, 7).astype(BF16)  14.3 us
  transfers between devices with their start and end apart: 45, of which 23 were waited for; matrix products, arithmetic and copies ran while one was open for 7% of the time, Pallas kernels for 18%

commit v1 on v0

--- a/solution.py
+++ b/solution.py
@@ -474,7 +474,7 @@
 
         def relay(first):
             second = swap(first, "dp", 0)
-            return first, second, core_swap(first), core_swap(second)
+            return first, second, core_swap(first), second
 
         fields_t = ((count, length, SLOT), BF16)
         probs_t = ((count, length, CLUSTER), BF16)
@@ -495,14 +495,16 @@
             near_attention, [fields_t, probs_t, ctx_t, rows_f, *orders_t], [*tables, raw, scores, columns], 8,
             where_arg, layer_input, packed, c1, small, small_1, segment_ids, after=(small_2,),
         )
-        small_3 = core_swap(tie(small_2, attn_sum))
+        small_3 = core_swap(small_2)
         c_far = relay(tie(c_first, attn_sum))
+        c_far = (*c_far[:3], core_swap(c_far[3]))
         u_far = relay(tie(u_first, attn_sum))
         far_fields, far_probs, far_ctx, *far_orders, low, normed_a, inverse_a = call(
             far_attention, [fields_t, probs_t, ctx_t, *orders_t, rows_b, rows_f, ((length, 1), F32)],
-            [*tables, raw, scores, columns, mat, mat, pltpu.VMEM((length, width), F32)], 9,
+            [*tables, raw, scores, columns, mat, mat, pltpu.VMEM((length, width), F32)], 1,
             where_arg, layer_input, *c_far, small_2, small_3, segment_ids, attn_sum, vecs,
         )
+        u_far = (*u_far[:3], core_swap(tie(u_far[3], low)))
         d_far = relay(tie(d_first, low))
         near_hidden, near_slope, ffn_sum = call(
             near_forward, [pair_b, pair_b, rows_f], [], 6, low, up_weight, u1, down_weight, d1, small, small_1
@@ -510,6 +512,7 @@
         far_hidden, far_slope = call(
             far_up, [pair_b, pair_b], [mat, mat], 5, where_arg, low, *u_far, small_2, small_3
         )
+        d_far = (*d_far[:3], core_swap(tie(d_far[3], ffn_sum, far_hidden)))
         layer_output, grad_b, grad_b_low, sums_b = call(
             far_down, [rows_b, rows_f, rows_b, vec_t], [mat, mat], 5,
             where_arg, far_hidden, *d_far, ffn_sum, normed_a, out_cotangent, vecs,
@@ -542,27 +545,39 @@
             layer_input, grad_a_low, packed, c1, *near_orders, near_fields, near_probs, near_ctx,
             sums_b, sums_a, near_ub, in_sum, grad_a, after=(down_total, packed_cross),
         )
-        up_total = add(add(ug0, us1), tie(chip_swap(up_cross), input_grad))
-        packed_total = add(add(cg0, core_swap(cg1)), chip_swap(packed_cross))
-
-        def reduce(total):
-            for level in range(levels):
+        steps = [(level, True) for level in range(levels)] + [(level, False) for level in reversed(range(levels))]
+
+        def step(total, at, *others):
+            level, halve = steps[at]
+            bit = (place >> level) & 1
+            if halve:
                 rows = total.shape[0] // 2
-                bit = (place >> level) & 1
                 send = lax.dynamic_slice_in_dim(total, (1 - bit) * rows, rows, axis=0)
                 keep = lax.dynamic_slice_in_dim(total, bit * rows, rows, axis=0)
-                total = add(keep, swap(send, "dp", level))
-            for level in reversed(range(levels)):
-                bit = (place >> level) & 1
-                other = swap(total, "dp", level)
-                total = jnp.where(
-                    bit == 0, jnp.concatenate([total, other], axis=0), jnp.concatenate([other, total], axis=0)
-                )
-            return total
-
-        down_grad = reduce(down_total).astype(F32)
-        up_grad = reduce(up_total).astype(F32)
-        packed_grad = reduce(packed_total)
+                return add(keep, tie(swap(send, "dp", level), *others))
+            other = tie(swap(total, "dp", level), *others)
+            return jnp.where(
+                bit == 0, jnp.concatenate([total, other], axis=0), jnp.concatenate([other, total], axis=0)
+            )
+
+        last = len(steps) - 1
+        down, up, whole = [down_total], [], []
+
+        def reach(chain, at, *others):
+            while len(chain) < min(at, last) + 2:
+                chain.append(step(chain[-1], len(chain) - 1, *others))
+            return chain[-1]
+
+        reach(down, 0, input_grad)
+        up.append(add(add(ug0, us1), tie(chip_swap(up_cross), down[-1])))
+        reach(down, 2)
+        reach(up, 0)
+        whole.append(add(add(cg0, core_swap(cg1)), tie(chip_swap(packed_cross), down[-1], up[-1])))
+        for at in range(last + 1):
+            reach(down, at + 4)
+            reach(up, at + 2)
+            reach(whole, at, down[-1], up[-1])
+        down_grad, up_grad, packed_grad = down[-1].astype(F32), up[-1].astype(F32), whole[-1]
         qkv_grad, out_grad, sums = call(
             unpack,
             [((3, width, heads * HEAD_DIM), F32), ((heads * HEAD_DIM, width), F32), ((16, width), F32)], [], 1,

time: 282 us -> 251 us (0.89)
  waiting for transfers between devices: 134 us -> 110 us
  starting transfers between devices: 41.8 us -> 33.8 us
    ppermute x45, waiting for transfers between devices: 134 us -> 110 us  [swap(): return lax.ppermute(v, axis, [(i, i ^ 1 << bit) for i in range(size)])]
    ppermute x45, starting transfers between devices: 41.8 us -> 33.8 us  [swap(): return lax.ppermute(v, axis, [(i, i ^ 1 << bit) for i in range(size)])]
    unnamed x129 -> x107, local copies, waits for them, and re-layouts: 17.6 us -> 19.2 us
  transfers between devices with their start and end apart: 45 -> 45, of which waited for: 23 -> 24; matrix products, arithmetic and copies ran while one was open for 7% -> 8% of each run, Pallas kernels for 18% -> 20%
where the time goes in v1:
time: 251 us; the launch traced here: 248 us
  waiting for transfers between devices  110 us (44%)
  Pallas kernels  60.5 us (24%)
  starting transfers between devices  33.8 us (13%)
  local copies, waits for them, and re-layouts  23.1 us (9%)
  other arithmetic  19.7 us (8%)
    ppermute x45, waiting for transfers between devices, swap(): return lax.ppermute(v, axis, [(i, i ^ 1 << bit) for i in range(size)])  110 us
    pallas_call x12, Pallas kernels, call(): pl.pallas_call(run, out_shape=shapes, in_specs=[placed(a) for a in args]...  60.5 us
    ppermute x45, starting transfers between devices, swap(): return lax.ppermute(v, axis, [(i, i ^ 1 << bit) for i in range(size)])  33.8 us
    unnamed x107, local copies, waits for them, and re-layouts  19.2 us
    convert_element_type x15, other arithmetic, add(): lax.reduce_precision(a.astype(F32) + b.astype(F32), 8, 7).astype(BF16)  14.4 us
  transfers between devices with their start and end apart: 45, of which 24 were waited for; matrix products, arithmetic and copies ran while one was open for 8% of the time, Pallas kernels for 20%

profile of v1, /device:TPU:0, one launch (start us, length us, event | category | flops | bytes accessed | tf_op | source)
XLA Modules:
  0.0 248.4 jit_solution(16012115479653545501)
XLA Ops:
  8.7 3.0 %collective-permute-start.3 = (f32[16,512]{1,0:T(8,128)S(1)}, f32[16,512]{1,0:T(8,128)S(1)}, u32[]{:S(2)}, u32[]{:S(2)}) collective-permute-start(f32[16,512]{1,0:T(8,128)S(1)} %get-tuple-element.83.refs_4_.refs_5_), channel_id=1, source_target_pairs={{0,2},{1,3},{2,0},{3,1},{4,6},{5,7},{6,4},{7,5},{8,10},{9,11},{10,... | collective-permute-start | bytes 98312 | tf_op jit(solution)/shard_map/ppermute | solution.py:426
  14.6 7.7 %shard_map.264 = (bf16[6,512,256]{2,1,0:T(8,128)(2,1)S(1)}, bf16[6,512,128]{2,1,0:T(8,128)(2,1)S(1)}, bf16[512,768]{1,0:T(8,128)(2,1)S(1)}, f32[512,768]{1,0:T(8...) custom-call(s32[2]{0:T(128)S(1)} %pad_add_fusion.refs_0_, bf16[512,768]{1,0:T(8,128)(2,1)S(1)} %copy-done, ...), custom_call_target="tpu_custom_call" | custom-call | flops 8000000000 | tf_op jit(solution)/shard_map/pallas_call | solution.py:49
  30.1 9.3 %collective-permute-done.8.refs_2_.refs_8_ = bf16[384,768]{1,0:T(8,128)(2,1)S(1)} collective-permute-done((bf16[384,768]{1,0:T(8,128)(2,1)S(1)}, bf16[384,768]{1,0:T(8,128)(2,1)S(1)}, u32[]{:S(2)}, u32[]{:S(2)}) %collective-permute-start.8) | collective-permute-done | bytes 589856 | tf_op jit(solution)/shard_map/ppermute | solution.py:426
  44.3 7.2 %shard_map.265 = (bf16[6,512,256]{2,1,0:T(8,128)(2,1)S(1)}, bf16[6,512,128]{2,1,0:T(8,128)(2,1)S(1)}, bf16[512,768]{1,0:T(8,128)(2,1)S(1)}, f32[8,512]{1,0:T(8,1...) custom-call(s32[2]{0:T(128)S(1)} %pad_add_fusion.refs_0_, ...), custom_call_target="tpu_custom_call" | custom-call | flops 1000000000 | tf_op jit(solution)/shard_map/pallas_call | solution.py:49
  51.5 4.5 %collective-permute-done.9.refs_3_.refs_9_ = bf16[384,768]{1,0:T(8,128)(2,1)S(1)} collective-permute-done((bf16[384,768]{1,0:T(8,128)(2,1)S(1)}, bf16[384,768]{1,0:T(8,128)(2,1)S(1)}, u32[]{:S(2)}, u32[]{:S(2)}) %collective-permute-start.9) | collective-permute-done | bytes 589856 | tf_op jit(solution)/shard_map/ppermute | solution.py:426
  58.6 3.1 %shard_map.267 = (bf16[2,512,768]{2,1,0:T(8,128)(2,1)S(1)}, bf16[2,512,768]{2,1,0:T(8,128)(2,1)S(1)}, f32[512,768]{1,0:T(8,128)S(1)}) custom-call(bf16[512,768]{1,0:T(8,128)(2,1)S(1)} %get-tuple-element.87.refs_1_.refs_0_.refs_2_, bf16[768,768]{1,0:T(8,128)(2,1)S(1)} %copy-done.3, bf16[768,768]{1,0:T(8,128)(2,1)S(1)} %collective-permute-done.15.refs_2_.refs_6_, ...), custom_call_target="tpu_custom_call" | custom-call | flops 6000000000 | tf_op jit(solution)/shard_map/pallas_call | solution.py:49
  64.3 8.7 %collective-permute-done.13.refs_3_.refs_5_ = bf16[384,768]{1,0:T(8,128)(2,1)S(1)} collective-permute-done((bf16[384,768]{1,0:T(8,128)(2,1)S(1)}, bf16[384,768]{1,0:T(8,128)(2,1)S(1)}, u32[]{:S(2)}, u32[]{:S(2)}) %collective-permute-start.13) | collective-permute-done | bytes 589856 | tf_op jit(solution)/shard_map/ppermute | solution.py:426
  75.0 3.7 %shard_map.268 = (bf16[512,768]{1,0:T(8,128)(2,1)}, f32[512,768]{1,0:T(8,128)S(1)}, bf16[512,768]{1,0:T(8,128)(2,1)S(1)}, f32[8,768]{1,0:T(8,128)S(1)}) custom-call(s32[2]{0:T(128)S(1)} %pad_add_fusion.refs_0_, bf16[2,512,768]{2,1,0:T(8,128)(2,1)S(1)} %get-tuple-element.90.refs_1_.refs_0_, bf16[384,768]{1,0:T(8,128)(2,1)S(1)} %collective-permute-done.12.refs_2_.refs_4_, ...), custom_call_target="tpu_custom_call" | custom-call | flops 5000000000 | tf_op jit(solution)/shard_map/pallas_call | solution.py:49
  78.7 3.3 %shard_map.270 = (bf16[768,768]{1,0:T(8,128)(2,1)S(1)}, bf16[768,768]{1,0:T(8,128)(2,1)S(1)}, bf16[768,768]{1,0:T(8,128)(2,1)}, bf16[768,768]{1,0:T(8,128)(2,1)S(1)}) custom-call(bf16[2,512,768]{2,1,0:T(8,128)(2,1)S(1)} %get-tuple-element.90.refs_1_.refs_0_, bf16[2,512,768]{2,1,0:T(8,128)(2,1)S(1)} %get-tuple-element.102.refs_1_, ...), custom_call_target="tpu_custom_call" | custom-call | flops 2800000000 | tf_op jit(solution)/shard_map/pallas_call | solution.py:49
  83.1 5.2 %shard_map.269 = (bf16[768,768]{1,0:T(8,128)(2,1)S(1)}, bf16[768,768]{1,0:T(8,128)(2,1)S(1)}, f32[512,768]{1,0:T(8,128)S(1)}, f32[8,768]{1,0:T(8,128)S(1)}) custom-call(s32[2]{0:T(128)S(1)} %pad_add_fusion.refs_0_, bf16[512,768]{1,0:T(8,128)(2,1)S(1)} %get-tuple-element.96.refs_1_.refs_2_.refs_0_, ...), custom_call_target="tpu_custom_call" | custom-call | flops 100000000 | tf_op jit(solution)/shard_map/pallas_call | solution.py:49
  90.0 4.9 %shard_map.271 = (bf16[768,768]{1,0:T(8,128)(2,1)S(1)}, bf16[768,768]{1,0:T(8,128)(2,1)S(1)}, f32[512,768]{1,0:T(8,128)S(1)}, bf16[512,768]{1,0:T(8,128)(2,1)S(1...) custom-call(bf16[512,768]{1,0:T(8,128)(2,1)S(1)} %get-tuple-element.96.refs_1_.refs_2_.refs_0_, ...), custom_call_target="tpu_custom_call" | custom-call | flops 100000000 | tf_op jit(solution)/shard_map/pallas_call | solution.py:49
  97.7 9.3 %shard_map.272 = (bf16[832,768]{1,0:T(8,128)(2,1)}, bf16[832,768]{1,0:T(8,128)(2,1)S(1)}, f32[512,768]{1,0:T(8,128)S(1)}) custom-call(s32[2]{0:T(128)S(1)} %copy-done.29, bf16[512,768]{1,0:T(8,128)(2,1)S(1)} %copy-done, bf16[512,768]{1,0:T(8,128)(2,1)S(1)} %get-tuple-element.106.refs_2_.refs_1_, bf16[384,768]{1,0:T(8,128)(2,1)S(1)} %copy-done.6, ...), custom_call_target="tpu_custom_call" | custom-call | flops 100000000 | tf_op jit(solution)/shard_map/pallas_call | solution.py:49
  110.9 7.2 %collective-permute-done.21 = bf16[768,768]{1,0:T(8,128)(2,1)} collective-permute-done((bf16[768,768]{1,0:T(8,128)(2,1)S(1)}, bf16[768,768]{1,0:T(8,128)(2,1)}, u32[]{:S(2)}, u32[]{:S(2)}) %collective-permute-start.21) | collective-permute-done | bytes 1179680 | tf_op jit(solution)/shard_map/ppermute | solution.py:426
  129.0 10.0 %shard_map.273 = (bf16[832,768]{1,0:T(8,128)(2,1)}, bf16[832,768]{1,0:T(8,128)(2,1)S(1)}, bf16[512,768]{1,0:T(8,128)(2,1)}) custom-call(bf16[512,768]{1,0:T(8,128)(2,1)S(1)} %copy-done, bf16[512,768]{1,0:T(8,128)(2,1)S(1)} %copy-done.2, bf16[768,768]{1,0:T(8,128)(2,1)} %get-tuple-element.82.refs_2_, bf16[768,768]{1,0:T(8,128)(2,1)} %collective-permute-done.1.refs_3_, ...), custom_call_target="tpu_custom_call" | custom-call | flops 100000000 | tf_op jit(solution)/shard_map/pallas_call | solution.py:49
  152.6 6.5 %collective-permute-done.27 = bf16[96,768]{1,0:T(8,128)(2,1)S(1)} collective-permute-done((bf16[96,768]{1,0:T(8,128)(2,1)S(1)}, bf16[96,768]{1,0:T(8,128)(2,1)S(1)}, u32[]{:S(2)}, u32[]{:S(2)}) %collective-permute-start.27) | collective-permute-done | bytes 147488 | tf_op jit(solution)/shard_map/ppermute | solution.py:426
  159.2 9.0 %collective-permute-done.32 = bf16[96,768]{1,0:T(8,128)(2,1)S(1)} collective-permute-done((bf16[96,768]{1,0:T(8,128)(2,1)S(1)}, bf16[96,768]{1,0:T(8,128)(2,1)S(1)}, u32[]{:S(2)}, u32[]{:S(2)}) %collective-permute-start.32) | collective-permute-done | bytes 147488 | tf_op jit(solution)/shard_map/ppermute | solution.py:426
  173.7 2.8 %collective-permute-done.34 = bf16[192,768]{1,0:T(8,128)(2,1)S(1)} collective-permute-done((bf16[192,768]{1,0:T(8,128)(2,1)S(1)}, bf16[192,768]{1,0:T(8,128)(2,1)S(1)}, u32[]{:S(2)}, u32[]{:S(2)}) %collective-permute-start.34) | collective-permute-done | bytes 294944 | tf_op jit(solution)/shard_map/ppermute | solution.py:426
  179.8 4.5 %collective-permute-done.35 = bf16[96,768]{1,0:T(8,128)(2,1)S(1)} collective-permute-done((bf16[96,768]{1,0:T(8,128)(2,1)S(1)}, bf16[96,768]{1,0:T(8,128)(2,1)S(1)}, u32[]{:S(2)}, u32[]{:S(2)}) %collective-permute-start.35) | collective-permute-done | bytes 147488 | tf_op jit(solution)/shard_map/ppermute | solution.py:426
  185.7 3.2 %collective-permute-done.33 = bf16[192,768]{1,0:T(8,128)(2,1)S(1)} collective-permute-done((bf16[192,768]{1,0:T(8,128)(2,1)S(1)}, bf16[192,768]{1,0:T(8,128)(2,1)S(1)}, u32[]{:S(2)}, u32[]{:S(2)}) %collective-permute-start.33) | collective-permute-done | bytes 294944 | tf_op jit(solution)/shard_map/ppermute | solution.py:426
  194.9 7.2 %collective-permute-done.40 = bf16[192,768]{1,0:T(8,128)(2,1)S(1)} collective-permute-done((bf16[192,768]{1,0:T(8,128)(2,1)S(1)}, bf16[192,768]{1,0:T(8,128)(2,1)S(1)}, u32[]{:S(2)}, u32[]{:S(2)}) %collective-permute-start.40) | collective-permute-done | bytes 294944 | tf_op jit(solution)/shard_map/ppermute | solution.py:426
  207.8 10.2 %collective-permute-done.39 = bf16[104,768]{1,0:T(8,128)(2,1)S(1)} collective-permute-done((bf16[104,768]{1,0:T(8,128)(2,1)S(1)}, bf16[104,768]{1,0:T(8,128)(2,1)S(1)}, u32[]{:S(2)}, u32[]{:S(2)}) %collective-permute-start.39) | collective-permute-done | bytes 159776 | tf_op jit(solution)/shard_map/ppermute | solution.py:426
  219.9 5.4 %collective-permute-done.41 = bf16[104,768]{1,0:T(8,128)(2,1)S(1)} collective-permute-done((bf16[104,768]{1,0:T(8,128)(2,1)S(1)}, bf16[104,768]{1,0:T(8,128)(2,1)S(1)}, u32[]{:S(2)}, u32[]{:S(2)}) %collective-permute-start.41) | collective-permute-done | bytes 159776 | tf_op jit(solution)/shard_map/ppermute | solution.py:426
  225.4 7.0 %collective-permute-done.43 = bf16[208,768]{1,0:T(8,128)(2,1)S(1)} collective-permute-done((bf16[208,768]{1,0:T(8,128)(2,1)S(1)}, bf16[208,768]{1,0:T(8,128)(2,1)S(1)}, u32[]{:S(2)}, u32[]{:S(2)}) %collective-permute-start.43) | collective-permute-done | bytes 319520 | tf_op jit(solution)/shard_map/ppermute | solution.py:426
  234.2 8.8 %collective-permute-done.44 = bf16[416,768]{1,0:T(8,128)(2,1)S(1)} collective-permute-done((bf16[416,768]{1,0:T(8,128)(2,1)S(1)}, bf16[416,768]{1,0:T(8,128)(2,1)S(1)}, u32[]{:S(2)}, u32[]{:S(2)}) %collective-permute-start.44) | collective-permute-done | bytes 639008 | tf_op jit(solution)/shard_map/ppermute | solution.py:426
  (232 shorter events, 95.1 us)
Async XLA Ops:
  11.6 16.4 %collective-permute-start = (bf16[384,768]{1,0:T(8,128)(2,1)}, bf16[384,768]{1,0:T(8,128)(2,1)S(1)}, u32[]{:S(2)}, u32[]{:S(2)}) collective-permute-start(bf16[384,768]{1,0:T(8,128)(2,1)} %get-tuple-element.81), channel_id=1, source_target_pairs={{0,2},{1,3},{2,0},{3,1},{4,6},{5,7},{6,4},{7,5},{8,10},{9,11},{10,... | collective-permute-start | bytes 1769480 | tf_op jit(solution)/shard_map/ppermute | solution.py:426
  11.7 27.7 %collective-permute-start.8 = (bf16[384,768]{1,0:T(8,128)(2,1)S(1)}, bf16[384,768]{1,0:T(8,128)(2,1)S(1)}, u32[]{:S(2)}, u32[]{:S(2)}) collective-permute-start(bf16[384,768]{1,0:T(8,128)(2,1)S(1)} %constant_dynamic-slice_fusion.10), channel_id=1, source_target_pairs={{0,2},{1,3},{2,0},{3,1},{4,6},{5,7},{6,4},{7,5},{8,10},{9,11},{10,... | collective-permute-start | bytes 1769480 | tf_op jit(solution)/shard_map/ppermute | solution.py:426
  28.1 14.1 %collective-permute-start.4 = (bf16[384,768]{1,0:T(8,128)(2,1)S(1)}, bf16[384,768]{1,0:T(8,128)(2,1)S(1)}, u32[]{:S(2)}, u32[]{:S(2)}) collective-permute-start(bf16[384,768]{1,0:T(8,128)(2,1)S(1)} %collective-permute-done.refs_2_.refs_3_), channel_id=1, source_target_pairs={{0,4},{4,0},{8,12},{12,8},{16,20},{20,16},{24,28},{28,24},{1,5},{5... | collective-permute-start | bytes 1769480 | tf_op jit(solution)/shard_map/ppermute | solution.py:426
  29.6 12.6 %collective-permute-start.5 = (bf16[384,768]{1,0:T(8,128)(2,1)S(1)}, bf16[384,768]{1,0:T(8,128)(2,1)S(1)}, u32[]{:S(2)}, u32[]{:S(2)}) collective-permute-start(bf16[384,768]{1,0:T(8,128)(2,1)S(1)} %collective-permute-done.refs_2_.refs_3_), channel_id=1, source_target_pairs={{0,1},{1,0},{2,3},{3,2},{4,5},{5,4},{6,7},{7,6},{8,9},{9,8},{10,11... | collective-permute-start | bytes 1769480 | tf_op jit(solution)/shard_map/ppermute | solution.py:426
  29.6 29.0 %collective-permute-start.15 = (bf16[768,768]{1,0:T(8,128)(2,1)S(1)}, bf16[768,768]{1,0:T(8,128)(2,1)S(1)}, u32[]{:S(2)}, u32[]{:S(2)}) collective-permute-start(bf16[768,768]{1,0:T(8,128)(2,1)S(1)} %copy-done.3), channel_id=1, source_target_pairs={{0,1},{1,0},{2,3},{3,2},{4,5},{5,4},{6,7},{7,6},{8,9},{9,8},{10,11... | collective-permute-start | bytes 3538952 | tf_op jit(solution)/shard_map/ppermute | solution.py:426
  30.1 28.5 %collective-permute-start.16 = (bf16[768,768]{1,0:T(8,128)(2,1)S(1)}, bf16[768,768]{1,0:T(8,128)(2,1)S(1)}, u32[]{:S(2)}, u32[]{:S(2)}) collective-permute-start(bf16[768,768]{1,0:T(8,128)(2,1)S(1)} %copy-done.4), channel_id=1, source_target_pairs={{0,1},{1,0},{2,3},{3,2},{4,5},{5,4},{6,7},{7,6},{8,9},{9,8},{10,11... | collective-permute-start | bytes 3538952 | tf_op jit(solution)/shard_map/ppermute | solution.py:426
  40.7 15.4 %collective-permute-start.9 = (bf16[384,768]{1,0:T(8,128)(2,1)S(1)}, bf16[384,768]{1,0:T(8,128)(2,1)S(1)}, u32[]{:S(2)}, u32[]{:S(2)}) collective-permute-start(bf16[384,768]{1,0:T(8,128)(2,1)S(1)} %collective-permute-done.8.refs_2_.refs_8_), channel_id=1, source_target_pairs={{0,4},{4,0},{8,12},{12,8},{16,20},{20,16},{24,28},{28,24},{1,5},{5... | collective-permute-start | bytes 1769480 | tf_op jit(solution)/shard_map/ppermute | solution.py:426
  42.2 15.8 %collective-permute-start.12 = (bf16[384,768]{1,0:T(8,128)(2,1)S(1)}, bf16[384,768]{1,0:T(8,128)(2,1)S(1)}, u32[]{:S(2)}, u32[]{:S(2)}) collective-permute-start(bf16[384,768]{1,0:T(8,128)(2,1)S(1)} %constant_dynamic-slice_fusion.9), channel_id=1, source_target_pairs={{0,2},{1,3},{2,0},{3,1},{4,6},{5,7},{6,4},{7,5},{8,10},{9,11},{10,... | collective-permute-start | bytes 1769480 | tf_op jit(solution)/shard_map/ppermute | solution.py:426
  44.2 17.6 %collective-permute-start.10 = (bf16[384,768]{1,0:T(8,128)(2,1)S(1)}, bf16[384,768]{1,0:T(8,128)(2,1)S(1)}, u32[]{:S(2)}, u32[]{:S(2)}) collective-permute-start(bf16[384,768]{1,0:T(8,128)(2,1)S(1)} %collective-permute-done.8.refs_2_.refs_8_), channel_id=1, source_target_pairs={{0,1},{1,0},{2,3},{3,2},{4,5},{5,4},{6,7},{7,6},{8,9},{9,8},{10,11... | collective-permute-start | bytes 1769480 | tf_op jit(solution)/shard_map/ppermute | solution.py:426
  58.0 15.0 %collective-permute-start.13 = (bf16[384,768]{1,0:T(8,128)(2,1)S(1)}, bf16[384,768]{1,0:T(8,128)(2,1)S(1)}, u32[]{:S(2)}, u32[]{:S(2)}) collective-permute-start(bf16[384,768]{1,0:T(8,128)(2,1)S(1)} %collective-permute-done.12.refs_2_.refs_4_), channel_id=1, source_target_pairs={{0,4},{4,0},{8,12},{12,8},{16,20},{20,16},{24,28},{28,24},{1,5},{5... | collective-permute-start | bytes 1769480 | tf_op jit(solution)/shard_map/ppermute | solution.py:426
  58.6 14.4 %collective-permute-start.14 = (bf16[384,768]{1,0:T(8,128)(2,1)S(1)}, bf16[384,768]{1,0:T(8,128)(2,1)S(1)}, u32[]{:S(2)}, u32[]{:S(2)}) collective-permute-start(bf16[384,768]{1,0:T(8,128)(2,1)S(1)} %collective-permute-done.12.refs_2_.refs_4_), channel_id=1, source_target_pairs={{0,1},{1,0},{2,3},{3,2},{4,5},{5,4},{6,7},{7,6},{8,9},{9,8},{10,11... | collective-permute-start | bytes 1769480 | tf_op jit(solution)/shard_map/ppermute | solution.py:426
  89.1 29.0 %collective-permute-start.21 = (bf16[768,768]{1,0:T(8,128)(2,1)S(1)}, bf16[768,768]{1,0:T(8,128)(2,1)}, u32[]{:S(2)}, u32[]{:S(2)}) collective-permute-start(bf16[768,768]{1,0:T(8,128)(2,1)S(1)} %reduce-precision_convert_fusion.8.refs_12_), channel_id=1, source_target_pairs={{0,2},{1,3},{2,0},{3,1},{4,6},{5,7},{6,4},{7,5},{8,10},{9,11},{10,... | collective-permute-start | bytes 3538952 | tf_op jit(solution)/shard_map/ppermute | solution.py:426
  90.0 28.1 %collective-permute-start.20 = (bf16[768,768]{1,0:T(8,128)(2,1)}, bf16[768,768]{1,0:T(8,128)(2,1)}, u32[]{:S(2)}, u32[]{:S(2)}) collective-permute-start(bf16[768,768]{1,0:T(8,128)(2,1)} %get-tuple-element.127), channel_id=1, source_target_pairs={{0,1},{1,0},{2,3},{3,2},{4,5},{5,4},{6,7},{7,6},{8,9},{9,8},{10,11... | collective-permute-start | bytes 3538952 | tf_op jit(solution)/shard_map/ppermute | solution.py:426
  109.2 12.7 %collective-permute-start.22 = (bf16[832,768]{1,0:T(8,128)(2,1)}, bf16[832,768]{1,0:T(8,128)(2,1)}, u32[]{:S(2)}, u32[]{:S(2)}) collective-permute-start(bf16[832,768]{1,0:T(8,128)(2,1)} %get-tuple-element.130), channel_id=1, source_target_pairs={{0,1},{1,0},{2,3},{3,2},{4,5},{5,4},{6,7},{7,6},{8,9},{9,8},{10,11... | collective-permute-start | bytes 3833864 | tf_op jit(solution)/shard_map/ppermute | solution.py:426
  109.7 33.6 %collective-permute-start.29 = (bf16[768,768]{1,0:T(8,128)(2,1)}, bf16[768,768]{1,0:T(8,128)(2,1)}, u32[]{:S(2)}, u32[]{:S(2)}) collective-permute-start(bf16[768,768]{1,0:T(8,128)(2,1)} %reduce-precision_convert_fusion.7.refs_15_), channel_id=1, source_target_pairs={{0,2},{1,3},{2,0},{3,1},{4,6},{5,7},{6,4},{7,5},{8,10},{9,11},{10,... | collective-permute-start | bytes 3538952 | tf_op jit(solution)/shard_map/ppermute | solution.py:426
  110.9 32.5 %collective-permute-start.28 = (bf16[768,768]{1,0:T(8,128)(2,1)}, bf16[768,768]{1,0:T(8,128)(2,1)}, u32[]{:S(2)}, u32[]{:S(2)}) collective-permute-start(bf16[768,768]{1,0:T(8,128)(2,1)} %copy-done.30), channel_id=1, source_target_pairs={{0,1},{1,0},{2,3},{3,2},{4,5},{5,4},{6,7},{7,6},{8,9},{9,8},{10,11... | collective-permute-start | bytes 3538952 | tf_op jit(solution)/shard_map/ppermute | solution.py:426
  121.4 17.7 %collective-permute-start.25 = (bf16[384,768]{1,0:T(8,128)(2,1)}, bf16[384,768]{1,0:T(8,128)(2,1)}, u32[]{:S(2)}, u32[]{:S(2)}) collective-permute-start(bf16[384,768]{1,0:T(8,128)(2,1)} %constant_dynamic-slice_fusion.8), channel_id=1, source_target_pairs={{0,4},{4,0},{8,12},{12,8},{16,20},{20,16},{24,28},{28,24},{1,5},{5... | collective-permute-start | bytes 1769480 | tf_op jit(solution)/shard_map/ppermute | solution.py:426
  124.1 45.8 %collective-permute-start.24 = (bf16[832,768]{1,0:T(8,128)(2,1)S(1)}, bf16[832,768]{1,0:T(8,128)(2,1)}, u32[]{:S(2)}, u32[]{:S(2)}) collective-permute-start(bf16[832,768]{1,0:T(8,128)(2,1)S(1)} %reduce-precision_convert_fusion.2.refs_15_), channel_id=1, source_target_pairs={{0,2},{1,3},{2,0},{3,1},{4,6},{5,7},{6,4},{7,5},{8,10},{9,11},{10,... | collective-permute-start | bytes 3833864 | tf_op jit(solution)/shard_map/ppermute | solution.py:426
  139.1 30.8 %collective-permute-start.23 = (bf16[832,768]{1,0:T(8,128)(2,1)}, bf16[832,768]{1,0:T(8,128)(2,1)}, u32[]{:S(2)}, u32[]{:S(2)}) collective-permute-start(bf16[832,768]{1,0:T(8,128)(2,1)} %get-tuple-element.133), channel_id=1, source_target_pairs={{0,1},{1,0},{2,3},{3,2},{4,5},{5,4},{6,7},{7,6},{8,9},{9,8},{10,11... | collective-permute-start | bytes 3833864 | tf_op jit(solution)/shard_map/ppermute | solution.py:426
  146.7 21.5 %collective-permute-start.30 = (bf16[384,768]{1,0:T(8,128)(2,1)}, bf16[384,768]{1,0:T(8,128)(2,1)}, u32[]{:S(2)}, u32[]{:S(2)}) collective-permute-start(bf16[384,768]{1,0:T(8,128)(2,1)} %constant_dynamic-slice_fusion.5), channel_id=1, source_target_pairs={{0,4},{4,0},{8,12},{12,8},{16,20},{20,16},{24,28},{28,24},{1,5},{5... | collective-permute-start | bytes 1769480 | tf_op jit(solution)/shard_map/ppermute | solution.py:426
  172.2 20.4 %collective-permute-start.31 = (bf16[416,768]{1,0:T(8,128)(2,1)S(1)}, bf16[416,768]{1,0:T(8,128)(2,1)S(1)}, u32[]{:S(2)}, u32[]{:S(2)}) collective-permute-start(bf16[416,768]{1,0:T(8,128)(2,1)S(1)} %constant_dynamic-slice_fusion.4), channel_id=1, source_target_pairs={{0,4},{4,0},{8,12},{12,8},{16,20},{20,16},{24,28},{28,24},{1,5},{5... | collective-permute-start | bytes 1916936 | tf_op jit(solution)/shard_map/ppermute | solution.py:426
  189.2 16.3 %collective-permute-start.37 = (bf16[384,768]{1,0:T(8,128)(2,1)S(1)}, bf16[384,768]{1,0:T(8,128)(2,1)S(1)}, u32[]{:S(2)}, u32[]{:S(2)}) collective-permute-start(bf16[384,768]{1,0:T(8,128)(2,1)S(1)} %maximum_select_fusion.4), channel_id=1, source_target_pairs={{0,4},{4,0},{8,12},{12,8},{16,20},{20,16},{24,28},{28,24},{1,5},{5... | collective-permute-start | bytes 1769480 | tf_op jit(solution)/shard_map/ppermute | solution.py:426
  192.8 14.3 %collective-permute-start.36 = (bf16[208,768]{1,0:T(8,128)(2,1)S(1)}, bf16[208,768]{1,0:T(8,128)(2,1)S(1)}, u32[]{:S(2)}, u32[]{:S(2)}) collective-permute-start(bf16[208,768]{1,0:T(8,128)(2,1)S(1)} %constant_dynamic-slice_fusion.1), channel_id=1, source_target_pairs={{0,8},{4,12},{8,0},{12,4},{16,24},{20,28},{24,16},{28,20},{1,9},{5... | collective-permute-start | bytes 958472 | tf_op jit(solution)/shard_map/ppermute | solution.py:426
  202.3 15.9 %collective-permute-start.42 = (bf16[384,768]{1,0:T(8,128)(2,1)S(1)}, bf16[384,768]{1,0:T(8,128)(2,1)S(1)}, u32[]{:S(2)}, u32[]{:S(2)}) collective-permute-start(bf16[384,768]{1,0:T(8,128)(2,1)S(1)} %maximum_select_fusion.5), channel_id=1, source_target_pairs={{0,4},{4,0},{8,12},{12,8},{16,20},{20,16},{24,28},{28,24},{1,5},{5... | collective-permute-start | bytes 1769480 | tf_op jit(solution)/shard_map/ppermute | solution.py:426
  (69 other events, 419.5 us)

commit v2 on v1

--- a/solution.py
+++ b/solution.py
@@ -35,7 +35,7 @@
     return lax.dot_general(a, b, (((0,), (0,)), ((), ())), preferred_element_type=F32)
 
 
-def call(body, outs, scratch, micros, *args, after=()):
+def call(body, outs, scratch, micros, *args, after=(), apart=0):
     shapes = [jax.ShapeDtypeStruct(s, t) for s, t in outs]
     kept = len(args)
 
@@ -50,7 +50,7 @@
         run,
         out_shape=shapes,
         in_specs=[placed(a) for a in args] + [pl.BlockSpec(memory_space=pl.ANY)] * len(after),
-        out_specs=[pl.BlockSpec(memory_space=pltpu.VMEM)] * len(outs),
+        out_specs=[pl.BlockSpec(memory_space=pltpu.HBM if i < apart else pltpu.VMEM) for i in range(len(outs))],
         scratch_shapes=scratch,
         cost_estimate=pl.CostEstimate(flops=int(micros * 1e9), bytes_accessed=0, transcendentals=0),
         compiler_params=pltpu.CompilerParams(vmem_limit_bytes=VMEM_LIMIT),
@@ -115,19 +115,29 @@
         small_ref[row + 1 : row + 2, :] = jnp.concatenate([line[:, length:], jnp.zeros((1, length - rest), F32)], axis=1)
 
 
-def unpack(packed_ref, qkv_ref, out_ref, vec_ref):
+def unpack(packed_ref, qkv_out_ref, out_ref, vec_ref, bias_ref, qkv_ref, sems):
     width = packed_ref.shape[1]
     heads = width // SLOT
-    rows = qkv_ref.shape[1]
+    rows = qkv_ref.shape[2]
 
     def field(at):
         return jnp.concatenate(
             [packed_ref[0:rows, h * SLOT + at * HEAD_DIM : h * SLOT + (at + 1) * HEAD_DIM] for h in range(heads)], axis=1
         ).astype(F32)
 
-    qkv_ref[0], qkv_ref[2], qkv_ref[1] = field(0), field(1), field(2)
+    copies = []
+    for at, member in enumerate((0, 2, 1)):
+        qkv_ref[member] = field(at).T
+        copies.append(pltpu.make_async_copy(qkv_ref.at[member], qkv_out_ref.at[member], sems.at[at]))
+        copies[-1].start()
     out_ref[...] = field(3).T
-    vec_ref[...] = packed_ref[rows : rows + 16, :].astype(F32)
+    vectors = packed_ref[rows : rows + 16, :].astype(F32)
+    vec_ref[...] = vectors
+    for member in range(2):
+        starts = [h * SLOT + member * HEAD_DIM for h in range(heads)]
+        bias_ref[member : member + 1, :] = jnp.concatenate([vectors[7:8, c : c + HEAD_DIM] for c in starts], axis=1)
+    for copy in copies:
+        copy.wait()
 
 
 def put_orders(where_ref, packs, seg_ref, order_ref, turned_ref):
@@ -571,22 +581,23 @@
         reach(down, 0, input_grad)
         up.append(add(add(ug0, us1), tie(chip_swap(up_cross), down[-1])))
         reach(down, 2)
-        reach(up, 0)
+        reach(up, 0, down[-1])
+        reach(down, 3, up[-1])
         whole.append(add(add(cg0, core_swap(cg1)), tie(chip_swap(packed_cross), down[-1], up[-1])))
         for at in range(last + 1):
-            reach(down, at + 4)
-            reach(up, at + 2)
+            reach(down, max(4, at + 3))
+            reach(up, at + 2 - (at > 1))
             reach(whole, at, down[-1], up[-1])
-        down_grad, up_grad, packed_grad = down[-1].astype(F32), up[-1].astype(F32), whole[-1]
-        qkv_grad, out_grad, sums = call(
+        down_grad, up_grad = [tie(chain[-1], whole[-2]).astype(F32) for chain in (down, up)]
+        packed_grad = whole[-1]
+        qkv_grad, out_grad, sums, qv_grad = call(
             unpack,
-            [((3, width, heads * HEAD_DIM), F32), ((heads * HEAD_DIM, width), F32), ((16, width), F32)], [], 1,
-            packed_grad,
-        )
-        field_sums = sums[7].reshape(heads, 4, HEAD_DIM)
-        qv_grad = jnp.stack([field_sums[:, 0].reshape(-1), field_sums[:, 1].reshape(-1)])
+            [((3, heads * HEAD_DIM, width), F32), ((heads * HEAD_DIM, width), F32), ((16, width), F32),
+             ((2, heads * HEAD_DIM), F32)],
+            [pltpu.VMEM((3, heads * HEAD_DIM, width), F32), pltpu.SemaphoreType.DMA((3,))], 1, packed_grad, apart=1,
+        )
         return (
-            layer_output, input_grad, qkv_grad, qv_grad, out_grad, sums[5], sums[3], sums[4],
+            layer_output, input_grad, qkv_grad.transpose(0, 2, 1), qv_grad, out_grad, sums[5], sums[3], sums[4],
             up_grad, sums[6], down_grad, sums[2], sums[0], sums[1],
         )
 

time: 251 us -> 249 us (level)
  waiting for transfers between devices: 110 us -> 96.1 us
  starting transfers between devices: 33.8 us -> 43.7 us
  other arithmetic: 19.7 us -> 22.6 us
    ppermute x45, waiting for transfers between devices: 110 us -> 96.1 us  [swap(): return lax.ppermute(v, axis, [(i, i ^ 1 << bit) for i in range(size)])]
    ppermute x45, starting transfers between devices: 33.8 us -> 43.7 us  [swap(): return lax.ppermute(v, axis, [(i, i ^ 1 << bit) for i in range(size)])]
    select_n x7 -> x9, other arithmetic: 1.42 us -> 4.58 us  [step(): jnp.where(bit == 0, jnp.concatenate([total, other], axis=0), jnp.concaten...]
    unnamed x107 -> x100, local copies, waits for them, and re-layouts: 19.2 us -> 17.1 us
  transfers between devices with their start and end apart: 45 -> 45, of which waited for: 24 -> 24; matrix products, arithmetic and copies ran while one was open for 8% -> 10% of each run, Pallas kernels for 20% -> 20%
where the time goes in v2:
time: 249 us; the launch traced here: 246 us
  waiting for transfers between devices  96.1 us (39%)
  Pallas kernels  61.7 us (25%)
  starting transfers between devices  43.7 us (18%)
  other arithmetic  22.6 us (9%)
  local copies, waits for them, and re-layouts  20.6 us (8%)
    ppermute x45, waiting for transfers between devices, swap(): return lax.ppermute(v, axis, [(i, i ^ 1 << bit) for i in range(size)])  96.1 us
    pallas_call x12, Pallas kernels, call(): pl.pallas_call(run, out_shape=shapes, in_specs=[placed(a) for a in args]...  61.7 us
    ppermute x45, starting transfers between devices, swap(): return lax.ppermute(v, axis, [(i, i ^ 1 << bit) for i in range(size)])  43.7 us
    unnamed x100, local copies, waits for them, and re-layouts  17.1 us
    convert_element_type x15, other arithmetic, add(): lax.reduce_precision(a.astype(F32) + b.astype(F32), 8, 7).astype(BF16)  14.8 us
  transfers between devices with their start and end apart: 45, of which 24 were waited for; matrix products, arithmetic and copies ran while one was open for 10% of the time, Pallas kernels for 20%

profile of v2, /device:TPU:0, one launch (start us, length us, event | category | flops | bytes accessed | tf_op | source)
XLA Modules:
  0.0 246.3 jit_solution(5316523038336143438)
XLA Ops:
  8.7 3.0 %collective-permute-start.3 = (f32[16,512]{1,0:T(8,128)S(1)}, f32[16,512]{1,0:T(8,128)S(1)}, u32[]{:S(2)}, u32[]{:S(2)}) collective-permute-start(f32[16,512]{1,0:T(8,128)S(1)} %get-tuple-element.88.refs_4_.refs_5_), channel_id=1, source_target_pairs={{0,2},{1,3},{2,0},{3,1},{4,6},{5,7},{6,4},{7,5},{8,10},{9,11},{10,... | collective-permute-start | bytes 98312 | tf_op jit(solution)/shard_map/ppermute | solution.py:436
  14.6 7.7 %shard_map.264 = (bf16[6,512,256]{2,1,0:T(8,128)(2,1)S(1)}, bf16[6,512,128]{2,1,0:T(8,128)(2,1)S(1)}, bf16[512,768]{1,0:T(8,128)(2,1)S(1)}, f32[512,768]{1,0:T(8...) custom-call(s32[2]{0:T(128)S(1)} %pad_add_fusion.refs_0_, bf16[512,768]{1,0:T(8,128)(2,1)S(1)} %copy-done, ...), custom_call_target="tpu_custom_call" | custom-call | flops 8000000000 | tf_op jit(solution)/shard_map/pallas_call | solution.py:49
  30.1 9.3 %collective-permute-done.8.refs_2_.refs_8_ = bf16[384,768]{1,0:T(8,128)(2,1)S(1)} collective-permute-done((bf16[384,768]{1,0:T(8,128)(2,1)S(1)}, bf16[384,768]{1,0:T(8,128)(2,1)S(1)}, u32[]{:S(2)}, u32[]{:S(2)}) %collective-permute-start.8) | collective-permute-done | bytes 589856 | tf_op jit(solution)/shard_map/ppermute | solution.py:436
  44.3 7.2 %shard_map.265 = (bf16[6,512,256]{2,1,0:T(8,128)(2,1)S(1)}, bf16[6,512,128]{2,1,0:T(8,128)(2,1)S(1)}, bf16[512,768]{1,0:T(8,128)(2,1)S(1)}, f32[8,512]{1,0:T(8,1...) custom-call(s32[2]{0:T(128)S(1)} %pad_add_fusion.refs_0_, ...), custom_call_target="tpu_custom_call" | custom-call | flops 1000000000 | tf_op jit(solution)/shard_map/pallas_call | solution.py:49
  51.5 4.5 %collective-permute-done.9.refs_3_.refs_9_ = bf16[384,768]{1,0:T(8,128)(2,1)S(1)} collective-permute-done((bf16[384,768]{1,0:T(8,128)(2,1)S(1)}, bf16[384,768]{1,0:T(8,128)(2,1)S(1)}, u32[]{:S(2)}, u32[]{:S(2)}) %collective-permute-start.9) | collective-permute-done | bytes 589856 | tf_op jit(solution)/shard_map/ppermute | solution.py:436
  58.6 3.1 %shard_map.267 = (bf16[2,512,768]{2,1,0:T(8,128)(2,1)S(1)}, bf16[2,512,768]{2,1,0:T(8,128)(2,1)S(1)}, f32[512,768]{1,0:T(8,128)S(1)}) custom-call(bf16[512,768]{1,0:T(8,128)(2,1)S(1)} %get-tuple-element.92.refs_1_.refs_0_.refs_2_, bf16[768,768]{1,0:T(8,128)(2,1)S(1)} %copy-done.3, bf16[768,768]{1,0:T(8,128)(2,1)S(1)} %collective-permute-done.15.refs_2_.refs_6_, ...), custom_call_target="tpu_custom_call" | custom-call | flops 6000000000 | tf_op jit(solution)/shard_map/pallas_call | solution.py:49
  64.3 8.7 %collective-permute-done.13.refs_3_.refs_5_ = bf16[384,768]{1,0:T(8,128)(2,1)S(1)} collective-permute-done((bf16[384,768]{1,0:T(8,128)(2,1)S(1)}, bf16[384,768]{1,0:T(8,128)(2,1)S(1)}, u32[]{:S(2)}, u32[]{:S(2)}) %collective-permute-start.13) | collective-permute-done | bytes 589856 | tf_op jit(solution)/shard_map/ppermute | solution.py:436
  75.0 3.7 %shard_map.268 = (bf16[512,768]{1,0:T(8,128)(2,1)}, f32[512,768]{1,0:T(8,128)S(1)}, bf16[512,768]{1,0:T(8,128)(2,1)S(1)}, f32[8,768]{1,0:T(8,128)S(1)}) custom-call(s32[2]{0:T(128)S(1)} %pad_add_fusion.refs_0_, bf16[2,512,768]{2,1,0:T(8,128)(2,1)S(1)} %get-tuple-element.95.refs_1_.refs_0_, bf16[384,768]{1,0:T(8,128)(2,1)S(1)} %collective-permute-done.12.refs_2_.refs_4_, ...), custom_call_target="tpu_custom_call" | custom-call | flops 5000000000 | tf_op jit(solution)/shard_map/pallas_call | solution.py:49
  78.7 3.3 %shard_map.270 = (bf16[768,768]{1,0:T(8,128)(2,1)S(1)}, bf16[768,768]{1,0:T(8,128)(2,1)S(1)}, bf16[768,768]{1,0:T(8,128)(2,1)}, bf16[768,768]{1,0:T(8,128)(2,1)S(1)}) custom-call(bf16[2,512,768]{2,1,0:T(8,128)(2,1)S(1)} %get-tuple-element.95.refs_1_.refs_0_, bf16[2,512,768]{2,1,0:T(8,128)(2,1)S(1)} %get-tuple-element.107.refs_1_, ...), custom_call_target="tpu_custom_call" | custom-call | flops 2800000000 | tf_op jit(solution)/shard_map/pallas_call | solution.py:49
  83.1 5.2 %shard_map.269 = (bf16[768,768]{1,0:T(8,128)(2,1)S(1)}, bf16[768,768]{1,0:T(8,128)(2,1)S(1)}, f32[512,768]{1,0:T(8,128)S(1)}, f32[8,768]{1,0:T(8,128)S(1)}) custom-call(s32[2]{0:T(128)S(1)} %pad_add_fusion.refs_0_, bf16[512,768]{1,0:T(8,128)(2,1)S(1)} %get-tuple-element.101.refs_1_.refs_2_.refs_0_, ...), custom_call_target="tpu_custom_call" | custom-call | flops 100000000 | tf_op jit(solution)/shard_map/pallas_call | solution.py:49
  90.0 4.9 %shard_map.271 = (bf16[768,768]{1,0:T(8,128)(2,1)S(1)}, bf16[768,768]{1,0:T(8,128)(2,1)S(1)}, f32[512,768]{1,0:T(8,128)S(1)}, bf16[512,768]{1,0:T(8,128)(2,1)S(1...) custom-call(bf16[512,768]{1,0:T(8,128)(2,1)S(1)} %get-tuple-element.101.refs_1_.refs_2_.refs_0_, ...), custom_call_target="tpu_custom_call" | custom-call | flops 100000000 | tf_op jit(solution)/shard_map/pallas_call | solution.py:49
  97.7 9.3 %shard_map.272 = (bf16[832,768]{1,0:T(8,128)(2,1)}, bf16[832,768]{1,0:T(8,128)(2,1)S(1)}, f32[512,768]{1,0:T(8,128)S(1)}) custom-call(s32[2]{0:T(128)S(1)} %copy-done.29, bf16[512,768]{1,0:T(8,128)(2,1)S(1)} %copy-done, bf16[512,768]{1,0:T(8,128)(2,1)S(1)} %get-tuple-element.111.refs_2_.refs_1_, bf16[384,768]{1,0:T(8,128)(2,1)S(1)} %copy-done.6, ...), custom_call_target="tpu_custom_call" | custom-call | flops 100000000 | tf_op jit(solution)/shard_map/pallas_call | solution.py:49
  110.9 7.1 %collective-permute-done.21 = bf16[768,768]{1,0:T(8,128)(2,1)} collective-permute-done((bf16[768,768]{1,0:T(8,128)(2,1)S(1)}, bf16[768,768]{1,0:T(8,128)(2,1)}, u32[]{:S(2)}, u32[]{:S(2)}) %collective-permute-start.21) | collective-permute-done | bytes 1179680 | tf_op jit(solution)/shard_map/ppermute | solution.py:436
  129.1 10.0 %shard_map.273 = (bf16[832,768]{1,0:T(8,128)(2,1)}, bf16[832,768]{1,0:T(8,128)(2,1)S(1)}, bf16[512,768]{1,0:T(8,128)(2,1)}) custom-call(bf16[512,768]{1,0:T(8,128)(2,1)S(1)} %copy-done, bf16[512,768]{1,0:T(8,128)(2,1)S(1)} %copy-done.2, bf16[768,768]{1,0:T(8,128)(2,1)} %get-tuple-element.87.refs_2_, bf16[768,768]{1,0:T(8,128)(2,1)} %collective-permute-done.1.refs_3_, ...), custom_call_target="tpu_custom_call" | custom-call | flops 100000000 | tf_op jit(solution)/shard_map/pallas_call | solution.py:49
  147.0 2.8 %collective-permute-done.26 = bf16[192,768]{1,0:T(8,128)(2,1)S(1)} collective-permute-done((bf16[192,768]{1,0:T(8,128)(2,1)S(1)}, bf16[192,768]{1,0:T(8,128)(2,1)S(1)}, u32[]{:S(2)}, u32[]{:S(2)}) %collective-permute-start.26) | collective-permute-done | bytes 294944 | tf_op jit(solution)/shard_map/ppermute | solution.py:436
  152.6 6.5 %collective-permute-done.27 = bf16[96,768]{1,0:T(8,128)(2,1)S(1)} collective-permute-done((bf16[96,768]{1,0:T(8,128)(2,1)S(1)}, bf16[96,768]{1,0:T(8,128)(2,1)S(1)}, u32[]{:S(2)}, u32[]{:S(2)}) %collective-permute-start.27) | collective-permute-done | bytes 147488 | tf_op jit(solution)/shard_map/ppermute | solution.py:436
  162.0 6.3 %collective-permute-done.28 = bf16[96,768]{1,0:T(8,128)(2,1)S(1)} collective-permute-done((bf16[96,768]{1,0:T(8,128)(2,1)S(1)}, bf16[96,768]{1,0:T(8,128)(2,1)S(1)}, u32[]{:S(2)}, u32[]{:S(2)}) %collective-permute-start.28) | collective-permute-done | bytes 147488 | tf_op jit(solution)/shard_map/ppermute | solution.py:436
  178.2 4.6 %collective-permute-done.35 = bf16[96,768]{1,0:T(8,128)(2,1)S(1)} collective-permute-done((bf16[96,768]{1,0:T(8,128)(2,1)S(1)}, bf16[96,768]{1,0:T(8,128)(2,1)S(1)}, u32[]{:S(2)}, u32[]{:S(2)}) %collective-permute-start.35) | collective-permute-done | bytes 147488 | tf_op jit(solution)/shard_map/ppermute | solution.py:436
  196.6 7.6 %collective-permute-done.41 = bf16[192,768]{1,0:T(8,128)(2,1)S(1)} collective-permute-done((bf16[192,768]{1,0:T(8,128)(2,1)S(1)}, bf16[192,768]{1,0:T(8,128)(2,1)S(1)}, u32[]{:S(2)}, u32[]{:S(2)}) %collective-permute-start.41) | collective-permute-done | bytes 294944 | tf_op jit(solution)/shard_map/ppermute | solution.py:436
  209.3 3.1 %collective-permute-done.38 = bf16[104,768]{1,0:T(8,128)(2,1)S(1)} collective-permute-done((bf16[104,768]{1,0:T(8,128)(2,1)S(1)}, bf16[104,768]{1,0:T(8,128)(2,1)S(1)}, u32[]{:S(2)}, u32[]{:S(2)}) %collective-permute-start.38) | collective-permute-done | bytes 159776 | tf_op jit(solution)/shard_map/ppermute | solution.py:436
  213.5 5.2 %collective-permute-done.40 = bf16[104,768]{1,0:T(8,128)(2,1)S(1)} collective-permute-done((bf16[104,768]{1,0:T(8,128)(2,1)S(1)}, bf16[104,768]{1,0:T(8,128)(2,1)S(1)}, u32[]{:S(2)}, u32[]{:S(2)}) %collective-permute-start.40) | collective-permute-done | bytes 159776 | tf_op jit(solution)/shard_map/ppermute | solution.py:436
  218.8 7.9 %collective-permute-start.42 = (bf16[208,768]{1,0:T(8,128)(2,1)S(1)}, bf16[208,768]{1,0:T(8,128)(2,1)S(1)}, u32[]{:S(2)}, u32[]{:S(2)}) collective-permute-start(bf16[208,768]{1,0:T(8,128)(2,1)S(1)} %maximum_select_fusion.6), channel_id=1, source_target_pairs={{0,8},{4,12},{8,0},{12,4},{16,24},{20,28},{24,16},{28,20},{1,9},{5... | collective-permute-start | bytes 958472 | tf_op jit(solution)/shard_map/ppermute | solution.py:436
  227.2 4.5 %collective-permute-done.42 = bf16[208,768]{1,0:T(8,128)(2,1)S(1)} collective-permute-done((bf16[208,768]{1,0:T(8,128)(2,1)S(1)}, bf16[208,768]{1,0:T(8,128)(2,1)S(1)}, u32[]{:S(2)}, u32[]{:S(2)}) %collective-permute-start.42) | collective-permute-done | bytes 319520 | tf_op jit(solution)/shard_map/ppermute | solution.py:436
  236.6 5.8 %collective-permute-done.44 = bf16[416,768]{1,0:T(8,128)(2,1)S(1)} collective-permute-done((bf16[416,768]{1,0:T(8,128)(2,1)S(1)}, bf16[416,768]{1,0:T(8,128)(2,1)S(1)}, u32[]{:S(2)}, u32[]{:S(2)}) %collective-permute-start.44) | collective-permute-done | bytes 639008 | tf_op jit(solution)/shard_map/ppermute | solution.py:436
  (222 shorter events, 103.3 us)
Async XLA Ops:
  11.6 16.4 %collective-permute-start = (bf16[384,768]{1,0:T(8,128)(2,1)}, bf16[384,768]{1,0:T(8,128)(2,1)S(1)}, u32[]{:S(2)}, u32[]{:S(2)}) collective-permute-start(bf16[384,768]{1,0:T(8,128)(2,1)} %get-tuple-element.86), channel_id=1, source_target_pairs={{0,2},{1,3},{2,0},{3,1},{4,6},{5,7},{6,4},{7,5},{8,10},{9,11},{10,... | collective-permute-start | bytes 1769480 | tf_op jit(solution)/shard_map/ppermute | solution.py:436
  11.7 27.7 %collective-permute-start.8 = (bf16[384,768]{1,0:T(8,128)(2,1)S(1)}, bf16[384,768]{1,0:T(8,128)(2,1)S(1)}, u32[]{:S(2)}, u32[]{:S(2)}) collective-permute-start(bf16[384,768]{1,0:T(8,128)(2,1)S(1)} %constant_dynamic-slice_fusion.10), channel_id=1, source_target_pairs={{0,2},{1,3},{2,0},{3,1},{4,6},{5,7},{6,4},{7,5},{8,10},{9,11},{10,... | collective-permute-start | bytes 1769480 | tf_op jit(solution)/shard_map/ppermute | solution.py:436
  28.1 14.1 %collective-permute-start.4 = (bf16[384,768]{1,0:T(8,128)(2,1)S(1)}, bf16[384,768]{1,0:T(8,128)(2,1)S(1)}, u32[]{:S(2)}, u32[]{:S(2)}) collective-permute-start(bf16[384,768]{1,0:T(8,128)(2,1)S(1)} %collective-permute-done.refs_2_.refs_3_), channel_id=1, source_target_pairs={{0,4},{4,0},{8,12},{12,8},{16,20},{20,16},{24,28},{28,24},{1,5},{5... | collective-permute-start | bytes 1769480 | tf_op jit(solution)/shard_map/ppermute | solution.py:436
  29.6 12.6 %collective-permute-start.5 = (bf16[384,768]{1,0:T(8,128)(2,1)S(1)}, bf16[384,768]{1,0:T(8,128)(2,1)S(1)}, u32[]{:S(2)}, u32[]{:S(2)}) collective-permute-start(bf16[384,768]{1,0:T(8,128)(2,1)S(1)} %collective-permute-done.refs_2_.refs_3_), channel_id=1, source_target_pairs={{0,1},{1,0},{2,3},{3,2},{4,5},{5,4},{6,7},{7,6},{8,9},{9,8},{10,11... | collective-permute-start | bytes 1769480 | tf_op jit(solution)/shard_map/ppermute | solution.py:436
  29.6 29.0 %collective-permute-start.15 = (bf16[768,768]{1,0:T(8,128)(2,1)S(1)}, bf16[768,768]{1,0:T(8,128)(2,1)S(1)}, u32[]{:S(2)}, u32[]{:S(2)}) collective-permute-start(bf16[768,768]{1,0:T(8,128)(2,1)S(1)} %copy-done.3), channel_id=1, source_target_pairs={{0,1},{1,0},{2,3},{3,2},{4,5},{5,4},{6,7},{7,6},{8,9},{9,8},{10,11... | collective-permute-start | bytes 3538952 | tf_op jit(solution)/shard_map/ppermute | solution.py:436
  30.1 28.5 %collective-permute-start.16 = (bf16[768,768]{1,0:T(8,128)(2,1)S(1)}, bf16[768,768]{1,0:T(8,128)(2,1)S(1)}, u32[]{:S(2)}, u32[]{:S(2)}) collective-permute-start(bf16[768,768]{1,0:T(8,128)(2,1)S(1)} %copy-done.4), channel_id=1, source_target_pairs={{0,1},{1,0},{2,3},{3,2},{4,5},{5,4},{6,7},{7,6},{8,9},{9,8},{10,11... | collective-permute-start | bytes 3538952 | tf_op jit(solution)/shard_map/ppermute | solution.py:436
  40.7 15.4 %collective-permute-start.9 = (bf16[384,768]{1,0:T(8,128)(2,1)S(1)}, bf16[384,768]{1,0:T(8,128)(2,1)S(1)}, u32[]{:S(2)}, u32[]{:S(2)}) collective-permute-start(bf16[384,768]{1,0:T(8,128)(2,1)S(1)} %collective-permute-done.8.refs_2_.refs_8_), channel_id=1, source_target_pairs={{0,4},{4,0},{8,12},{12,8},{16,20},{20,16},{24,28},{28,24},{1,5},{5... | collective-permute-start | bytes 1769480 | tf_op jit(solution)/shard_map/ppermute | solution.py:436
  42.2 15.8 %collective-permute-start.12 = (bf16[384,768]{1,0:T(8,128)(2,1)S(1)}, bf16[384,768]{1,0:T(8,128)(2,1)S(1)}, u32[]{:S(2)}, u32[]{:S(2)}) collective-permute-start(bf16[384,768]{1,0:T(8,128)(2,1)S(1)} %constant_dynamic-slice_fusion.9), channel_id=1, source_target_pairs={{0,2},{1,3},{2,0},{3,1},{4,6},{5,7},{6,4},{7,5},{8,10},{9,11},{10,... | collective-permute-start | bytes 1769480 | tf_op jit(solution)/shard_map/ppermute | solution.py:436
  44.2 17.6 %collective-permute-start.10 = (bf16[384,768]{1,0:T(8,128)(2,1)S(1)}, bf16[384,768]{1,0:T(8,128)(2,1)S(1)}, u32[]{:S(2)}, u32[]{:S(2)}) collective-permute-start(bf16[384,768]{1,0:T(8,128)(2,1)S(1)} %collective-permute-done.8.refs_2_.refs_8_), channel_id=1, source_target_pairs={{0,1},{1,0},{2,3},{3,2},{4,5},{5,4},{6,7},{7,6},{8,9},{9,8},{10,11... | collective-permute-start | bytes 1769480 | tf_op jit(solution)/shard_map/ppermute | solution.py:436
  58.0 15.0 %collective-permute-start.13 = (bf16[384,768]{1,0:T(8,128)(2,1)S(1)}, bf16[384,768]{1,0:T(8,128)(2,1)S(1)}, u32[]{:S(2)}, u32[]{:S(2)}) collective-permute-start(bf16[384,768]{1,0:T(8,128)(2,1)S(1)} %collective-permute-done.12.refs_2_.refs_4_), channel_id=1, source_target_pairs={{0,4},{4,0},{8,12},{12,8},{16,20},{20,16},{24,28},{28,24},{1,5},{5... | collective-permute-start | bytes 1769480 | tf_op jit(solution)/shard_map/ppermute | solution.py:436
  58.6 14.4 %collective-permute-start.14 = (bf16[384,768]{1,0:T(8,128)(2,1)S(1)}, bf16[384,768]{1,0:T(8,128)(2,1)S(1)}, u32[]{:S(2)}, u32[]{:S(2)}) collective-permute-start(bf16[384,768]{1,0:T(8,128)(2,1)S(1)} %collective-permute-done.12.refs_2_.refs_4_), channel_id=1, source_target_pairs={{0,1},{1,0},{2,3},{3,2},{4,5},{5,4},{6,7},{7,6},{8,9},{9,8},{10,11... | collective-permute-start | bytes 1769480 | tf_op jit(solution)/shard_map/ppermute | solution.py:436
  89.1 29.0 %collective-permute-start.21 = (bf16[768,768]{1,0:T(8,128)(2,1)S(1)}, bf16[768,768]{1,0:T(8,128)(2,1)}, u32[]{:S(2)}, u32[]{:S(2)}) collective-permute-start(bf16[768,768]{1,0:T(8,128)(2,1)S(1)} %reduce-precision_convert_fusion.8.refs_12_), channel_id=1, source_target_pairs={{0,2},{1,3},{2,0},{3,1},{4,6},{5,7},{6,4},{7,5},{8,10},{9,11},{10,... | collective-permute-start | bytes 3538952 | tf_op jit(solution)/shard_map/ppermute | solution.py:436
  90.0 28.1 %collective-permute-start.20 = (bf16[768,768]{1,0:T(8,128)(2,1)}, bf16[768,768]{1,0:T(8,128)(2,1)}, u32[]{:S(2)}, u32[]{:S(2)}) collective-permute-start(bf16[768,768]{1,0:T(8,128)(2,1)} %get-tuple-element.132), channel_id=1, source_target_pairs={{0,1},{1,0},{2,3},{3,2},{4,5},{5,4},{6,7},{7,6},{8,9},{9,8},{10,11... | collective-permute-start | bytes 3538952 | tf_op jit(solution)/shard_map/ppermute | solution.py:436
  109.2 12.7 %collective-permute-start.22 = (bf16[832,768]{1,0:T(8,128)(2,1)}, bf16[832,768]{1,0:T(8,128)(2,1)}, u32[]{:S(2)}, u32[]{:S(2)}) collective-permute-start(bf16[832,768]{1,0:T(8,128)(2,1)} %get-tuple-element.135), channel_id=1, source_target_pairs={{0,1},{1,0},{2,3},{3,2},{4,5},{5,4},{6,7},{7,6},{8,9},{9,8},{10,11... | collective-permute-start | bytes 3833864 | tf_op jit(solution)/shard_map/ppermute | solution.py:436
  109.7 33.6 %collective-permute-start.30 = (bf16[768,768]{1,0:T(8,128)(2,1)}, bf16[768,768]{1,0:T(8,128)(2,1)}, u32[]{:S(2)}, u32[]{:S(2)}) collective-permute-start(bf16[768,768]{1,0:T(8,128)(2,1)} %reduce-precision_convert_fusion.7.refs_15_), channel_id=1, source_target_pairs={{0,2},{1,3},{2,0},{3,1},{4,6},{5,7},{6,4},{7,5},{8,10},{9,11},{10,... | collective-permute-start | bytes 3538952 | tf_op jit(solution)/shard_map/ppermute | solution.py:436
  110.9 32.4 %collective-permute-start.29 = (bf16[768,768]{1,0:T(8,128)(2,1)}, bf16[768,768]{1,0:T(8,128)(2,1)}, u32[]{:S(2)}, u32[]{:S(2)}) collective-permute-start(bf16[768,768]{1,0:T(8,128)(2,1)} %copy-done.30), channel_id=1, source_target_pairs={{0,1},{1,0},{2,3},{3,2},{4,5},{5,4},{6,7},{7,6},{8,9},{9,8},{10,11... | collective-permute-start | bytes 3538952 | tf_op jit(solution)/shard_map/ppermute | solution.py:436
  121.4 17.7 %collective-permute-start.25 = (bf16[384,768]{1,0:T(8,128)(2,1)}, bf16[384,768]{1,0:T(8,128)(2,1)}, u32[]{:S(2)}, u32[]{:S(2)}) collective-permute-start(bf16[384,768]{1,0:T(8,128)(2,1)} %constant_dynamic-slice_fusion.8), channel_id=1, source_target_pairs={{0,4},{4,0},{8,12},{12,8},{16,20},{20,16},{24,28},{28,24},{1,5},{5... | collective-permute-start | bytes 1769480 | tf_op jit(solution)/shard_map/ppermute | solution.py:436
  124.1 45.8 %collective-permute-start.24 = (bf16[832,768]{1,0:T(8,128)(2,1)S(1)}, bf16[832,768]{1,0:T(8,128)(2,1)}, u32[]{:S(2)}, u32[]{:S(2)}) collective-permute-start(bf16[832,768]{1,0:T(8,128)(2,1)S(1)} %reduce-precision_convert_fusion.2.refs_15_), channel_id=1, source_target_pairs={{0,2},{1,3},{2,0},{3,1},{4,6},{5,7},{6,4},{7,5},{8,10},{9,11},{10,... | collective-permute-start | bytes 3833864 | tf_op jit(solution)/shard_map/ppermute | solution.py:436
  139.1 30.8 %collective-permute-start.23 = (bf16[832,768]{1,0:T(8,128)(2,1)}, bf16[832,768]{1,0:T(8,128)(2,1)}, u32[]{:S(2)}, u32[]{:S(2)}) collective-permute-start(bf16[832,768]{1,0:T(8,128)(2,1)} %get-tuple-element.138), channel_id=1, source_target_pairs={{0,1},{1,0},{2,3},{3,2},{4,5},{5,4},{6,7},{7,6},{8,9},{9,8},{10,11... | collective-permute-start | bytes 3833864 | tf_op jit(solution)/shard_map/ppermute | solution.py:436
  146.4 14.4 %collective-permute-start.31 = (bf16[384,768]{1,0:T(8,128)(2,1)}, bf16[384,768]{1,0:T(8,128)(2,1)}, u32[]{:S(2)}, u32[]{:S(2)}) collective-permute-start(bf16[384,768]{1,0:T(8,128)(2,1)} %constant_dynamic-slice_fusion.5), channel_id=1, source_target_pairs={{0,4},{4,0},{8,12},{12,8},{16,20},{20,16},{24,28},{28,24},{1,5},{5... | collective-permute-start | bytes 1769480 | tf_op jit(solution)/shard_map/ppermute | solution.py:436
  172.3 19.3 %collective-permute-start.32 = (bf16[416,768]{1,0:T(8,128)(2,1)S(1)}, bf16[416,768]{1,0:T(8,128)(2,1)S(1)}, u32[]{:S(2)}, u32[]{:S(2)}) collective-permute-start(bf16[416,768]{1,0:T(8,128)(2,1)S(1)} %constant_dynamic-slice_fusion.4), channel_id=1, source_target_pairs={{0,4},{4,0},{8,12},{12,8},{16,20},{20,16},{24,28},{28,24},{1,5},{5... | collective-permute-start | bytes 1916936 | tf_op jit(solution)/shard_map/ppermute | solution.py:436
  195.1 13.7 %collective-permute-start.39 = (bf16[384,768]{1,0:T(8,128)(2,1)S(1)}, bf16[384,768]{1,0:T(8,128)(2,1)S(1)}, u32[]{:S(2)}, u32[]{:S(2)}) collective-permute-start(bf16[384,768]{1,0:T(8,128)(2,1)S(1)} %maximum_select_fusion.4), channel_id=1, source_target_pairs={{0,4},{4,0},{8,12},{12,8},{16,20},{20,16},{24,28},{28,24},{1,5},{5... | collective-permute-start | bytes 1769480 | tf_op jit(solution)/shard_map/ppermute | solution.py:436
  207.3 19.4 %collective-permute-start.43 = (bf16[384,768]{1,0:T(8,128)(2,1)S(1)}, bf16[384,768]{1,0:T(8,128)(2,1)S(1)}, u32[]{:S(2)}, u32[]{:S(2)}) collective-permute-start(bf16[384,768]{1,0:T(8,128)(2,1)S(1)} %maximum_select_fusion.5), channel_id=1, source_target_pairs={{0,4},{4,0},{8,12},{12,8},{16,20},{20,16},{24,28},{28,24},{1,5},{5... | collective-permute-start | bytes 1769480 | tf_op jit(solution)/shard_map/ppermute | solution.py:436
  218.8 12.9 %collective-permute-start.42 = (bf16[208,768]{1,0:T(8,128)(2,1)S(1)}, bf16[208,768]{1,0:T(8,128)(2,1)S(1)}, u32[]{:S(2)}, u32[]{:S(2)}) collective-permute-start(bf16[208,768]{1,0:T(8,128)(2,1)S(1)} %maximum_select_fusion.6), channel_id=1, source_target_pairs={{0,8},{4,12},{8,0},{12,4},{16,24},{20,28},{24,16},{28,20},{1,9},{5... | collective-permute-start | bytes 958472 | tf_op jit(solution)/shard_map/ppermute | solution.py:436
  (66 other events, 414.2 us)

commit v3 on v2

--- a/solution.py
+++ b/solution.py
@@ -18,7 +18,7 @@
 PAIR = 2 * HEAD_DIM
 BLOCK = 128
 VMEM_LIMIT = 30 * 1024 * 1024
-EXTRA = 64
+EXTRA = 32
 F32 = jnp.float32
 BF16 = jnp.bfloat16
 
@@ -397,7 +397,7 @@
             ).astype(BF16)
         fields = colsum(tok_ref[group].astype(F32))
         block = jnp.concatenate([sums_b_ref[0:3, :], sums_a_ref[0:3, :], shift_ref[group : group + 1, :], fields], axis=0)
-        zero = jnp.zeros((EXTRA - 8, width), F32)
+        zero = jnp.zeros((out_ref.shape[0] - width - 8, width), F32)
         out_ref[width:, :] = jnp.concatenate([block, zero], axis=0).astype(BF16)
 
 
@@ -492,7 +492,7 @@
         orders_t = [((8, length), F32), ((length, 8), F32)]
         rows_f, rows_b = ((length, width), F32), ((length, width), BF16)
         pair_b = ((2, length, units), BF16)
-        tall = ((width + EXTRA, heads * SLOT), BF16)
+        tall = ((width + max(EXTRA, dp_size), heads * SLOT), BF16)
         mat, rows_s = pltpu.VMEM((width, width), BF16), pltpu.VMEM((length, width), BF16)
         tables = [pltpu.VMEM((count, length, length), BF16)] * 2
         columns = pltpu.VMEM((width, count * PAIR), BF16)

time: 249 us -> 248 us (level)
  waiting for transfers between devices: 96.1 us -> 109 us
  starting transfers between devices: 43.7 us -> 32.5 us
    ppermute x45, waiting for transfers between devices: 96.1 us -> 109 us  [swap(): return lax.ppermute(v, axis, [(i, i ^ 1 << bit) for i in range(size)])]
    ppermute x45, starting transfers between devices: 43.7 us -> 32.5 us  [swap(): return lax.ppermute(v, axis, [(i, i ^ 1 << bit) for i in range(size)])]
    unnamed x100 -> x82, local copies, waits for them, and re-layouts: 17.1 us -> 15.1 us
  transfers between devices with their start and end apart: 45 -> 45, of which waited for: 24 -> 24; matrix products, arithmetic and copies ran while one was open for 10% -> 9% of each run, Pallas kernels for 20% -> 20%
where the time goes in v3:
time: 248 us; the launch traced here: 245 us
  waiting for transfers between devices  109 us (44%)
  Pallas kernels  61.7 us (25%)
  starting transfers between devices  32.5 us (13%)
  other arithmetic  21.8 us (9%)
  local copies, waits for them, and re-layouts  18.6 us (8%)
    ppermute x45, waiting for transfers between devices, swap(): return lax.ppermute(v, axis, [(i, i ^ 1 << bit) for i in range(size)])  109 us
    pallas_call x12, Pallas kernels, call(): pl.pallas_call(run, out_shape=shapes, in_specs=[placed(a) for a in args]...  61.7 us
    ppermute x45, starting transfers between devices, swap(): return lax.ppermute(v, axis, [(i, i ^ 1 << bit) for i in range(size)])  32.5 us
    unnamed x82, local copies, waits for them, and re-layouts  15.1 us
    convert_element_type x15, other arithmetic, add(): lax.reduce_precision(a.astype(F32) + b.astype(F32), 8, 7).astype(BF16)  14.2 us
  transfers between devices with their start and end apart: 45, of which 24 were waited for; matrix products, arithmetic and copies ran while one was open for 9% of the time, Pallas kernels for 20%

profile of v3, /device:TPU:0, one launch (start us, length us, event | category | flops | bytes accessed | tf_op | source)
XLA Modules:
  0.0 244.7 jit_solution(7253684932183649169)
XLA Ops:
  8.7 3.0 %collective-permute-start.3 = (f32[16,512]{1,0:T(8,128)S(1)}, f32[16,512]{1,0:T(8,128)S(1)}, u32[]{:S(2)}, u32[]{:S(2)}) collective-permute-start(f32[16,512]{1,0:T(8,128)S(1)} %get-tuple-element.88.refs_4_.refs_5_), channel_id=1, source_target_pairs={{0,2},{1,3},{2,0},{3,1},{4,6},{5,7},{6,4},{7,5},{8,10},{9,11},{10,... | collective-permute-start | bytes 98312 | tf_op jit(solution)/shard_map/ppermute | solution.py:436
  13.8 7.7 %shard_map.264 = (bf16[6,512,256]{2,1,0:T(8,128)(2,1)S(1)}, bf16[6,512,128]{2,1,0:T(8,128)(2,1)S(1)}, bf16[512,768]{1,0:T(8,128)(2,1)S(1)}, f32[512,768]{1,0:T(8...) custom-call(s32[2]{0:T(128)S(1)} %pad_add_fusion.refs_0_, bf16[512,768]{1,0:T(8,128)(2,1)S(1)} %copy-done, ...), custom_call_target="tpu_custom_call" | custom-call | flops 8000000000 | tf_op jit(solution)/shard_map/pallas_call | solution.py:49
  24.4 3.7 %collective-permute-done.refs_2_.refs_3_ = bf16[384,768]{1,0:T(8,128)(2,1)S(1)} collective-permute-done((bf16[384,768]{1,0:T(8,128)(2,1)}, bf16[384,768]{1,0:T(8,128)(2,1)S(1)}, u32[]{:S(2)}, u32[]{:S(2)}) %collective-permute-start) | collective-permute-done | bytes 589856 | tf_op jit(solution)/shard_map/ppermute | solution.py:436
  30.1 9.3 %collective-permute-done.8.refs_2_.refs_8_ = bf16[384,768]{1,0:T(8,128)(2,1)S(1)} collective-permute-done((bf16[384,768]{1,0:T(8,128)(2,1)S(1)}, bf16[384,768]{1,0:T(8,128)(2,1)S(1)}, u32[]{:S(2)}, u32[]{:S(2)}) %collective-permute-start.8) | collective-permute-done | bytes 589856 | tf_op jit(solution)/shard_map/ppermute | solution.py:436
  44.3 7.2 %shard_map.265 = (bf16[6,512,256]{2,1,0:T(8,128)(2,1)S(1)}, bf16[6,512,128]{2,1,0:T(8,128)(2,1)S(1)}, bf16[512,768]{1,0:T(8,128)(2,1)S(1)}, f32[8,512]{1,0:T(8,1...) custom-call(s32[2]{0:T(128)S(1)} %pad_add_fusion.refs_0_, ...), custom_call_target="tpu_custom_call" | custom-call | flops 1000000000 | tf_op jit(solution)/shard_map/pallas_call | solution.py:49
  51.5 4.5 %collective-permute-done.9.refs_3_.refs_9_ = bf16[384,768]{1,0:T(8,128)(2,1)S(1)} collective-permute-done((bf16[384,768]{1,0:T(8,128)(2,1)S(1)}, bf16[384,768]{1,0:T(8,128)(2,1)S(1)}, u32[]{:S(2)}, u32[]{:S(2)}) %collective-permute-start.9) | collective-permute-done | bytes 589856 | tf_op jit(solution)/shard_map/ppermute | solution.py:436
  58.6 3.2 %shard_map.267 = (bf16[2,512,768]{2,1,0:T(8,128)(2,1)S(1)}, bf16[2,512,768]{2,1,0:T(8,128)(2,1)S(1)}, f32[512,768]{1,0:T(8,128)S(1)}) custom-call(bf16[512,768]{1,0:T(8,128)(2,1)S(1)} %get-tuple-element.92.refs_1_.refs_0_.refs_2_, bf16[768,768]{1,0:T(8,128)(2,1)S(1)} %copy-done.3, bf16[768,768]{1,0:T(8,128)(2,1)S(1)} %collective-permute-done.15.refs_2_.refs_6_, ...), custom_call_target="tpu_custom_call" | custom-call | flops 6000000000 | tf_op jit(solution)/shard_map/pallas_call | solution.py:49
  64.3 8.7 %collective-permute-done.13.refs_3_.refs_5_ = bf16[384,768]{1,0:T(8,128)(2,1)S(1)} collective-permute-done((bf16[384,768]{1,0:T(8,128)(2,1)S(1)}, bf16[384,768]{1,0:T(8,128)(2,1)S(1)}, u32[]{:S(2)}, u32[]{:S(2)}) %collective-permute-start.13) | collective-permute-done | bytes 589856 | tf_op jit(solution)/shard_map/ppermute | solution.py:436
  75.0 3.7 %shard_map.268 = (bf16[512,768]{1,0:T(8,128)(2,1)}, f32[512,768]{1,0:T(8,128)S(1)}, bf16[512,768]{1,0:T(8,128)(2,1)S(1)}, f32[8,768]{1,0:T(8,128)S(1)}) custom-call(s32[2]{0:T(128)S(1)} %pad_add_fusion.refs_0_, bf16[2,512,768]{2,1,0:T(8,128)(2,1)S(1)} %get-tuple-element.95.refs_1_.refs_0_, bf16[384,768]{1,0:T(8,128)(2,1)S(1)} %collective-permute-done.12.refs_2_.refs_4_, ...), custom_call_target="tpu_custom_call" | custom-call | flops 5000000000 | tf_op jit(solution)/shard_map/pallas_call | solution.py:49
  78.7 3.3 %shard_map.270 = (bf16[768,768]{1,0:T(8,128)(2,1)S(1)}, bf16[768,768]{1,0:T(8,128)(2,1)S(1)}, bf16[768,768]{1,0:T(8,128)(2,1)}, bf16[768,768]{1,0:T(8,128)(2,1)S(1)}) custom-call(bf16[2,512,768]{2,1,0:T(8,128)(2,1)S(1)} %get-tuple-element.95.refs_1_.refs_0_, bf16[2,512,768]{2,1,0:T(8,128)(2,1)S(1)} %get-tuple-element.107.refs_1_, ...), custom_call_target="tpu_custom_call" | custom-call | flops 2800000000 | tf_op jit(solution)/shard_map/pallas_call | solution.py:49
  83.1 5.2 %shard_map.269 = (bf16[768,768]{1,0:T(8,128)(2,1)S(1)}, bf16[768,768]{1,0:T(8,128)(2,1)S(1)}, f32[512,768]{1,0:T(8,128)S(1)}, f32[8,768]{1,0:T(8,128)S(1)}) custom-call(s32[2]{0:T(128)S(1)} %pad_add_fusion.refs_0_, bf16[512,768]{1,0:T(8,128)(2,1)S(1)} %get-tuple-element.101.refs_1_.refs_2_.refs_0_, ...), custom_call_target="tpu_custom_call" | custom-call | flops 100000000 | tf_op jit(solution)/shard_map/pallas_call | solution.py:49
  90.0 4.9 %shard_map.271 = (bf16[768,768]{1,0:T(8,128)(2,1)S(1)}, bf16[768,768]{1,0:T(8,128)(2,1)S(1)}, f32[512,768]{1,0:T(8,128)S(1)}, bf16[512,768]{1,0:T(8,128)(2,1)S(1...) custom-call(bf16[512,768]{1,0:T(8,128)(2,1)S(1)} %get-tuple-element.101.refs_1_.refs_2_.refs_0_, ...), custom_call_target="tpu_custom_call" | custom-call | flops 100000000 | tf_op jit(solution)/shard_map/pallas_call | solution.py:49
  97.0 9.3 %shard_map.272 = (bf16[800,768]{1,0:T(8,128)(2,1)}, bf16[800,768]{1,0:T(8,128)(2,1)S(1)}, f32[512,768]{1,0:T(8,128)S(1)}) custom-call(s32[2]{0:T(128)S(1)} %pad_add_fusion.refs_0_, bf16[512,768]{1,0:T(8,128)(2,1)S(1)} %copy-done, bf16[512,768]{1,0:T(8,128)(2,1)S(1)} %get-tuple-element.111.refs_2_.refs_1_, bf16[384,768]{1,0:T(8,128)(2,1)S(1)} %copy-done.6, ...), custom_call_target="tpu_custom_call" | custom-call | flops 100000000 | tf_op jit(solution)/shard_map/pallas_call | solution.py:49
  110.2 7.8 %collective-permute-done.21 = bf16[768,768]{1,0:T(8,128)(2,1)} collective-permute-done((bf16[768,768]{1,0:T(8,128)(2,1)S(1)}, bf16[768,768]{1,0:T(8,128)(2,1)}, u32[]{:S(2)}, u32[]{:S(2)}) %collective-permute-start.21) | collective-permute-done | bytes 1179680 | tf_op jit(solution)/shard_map/ppermute | solution.py:436
  128.9 10.0 %shard_map.273 = (bf16[800,768]{1,0:T(8,128)(2,1)}, bf16[800,768]{1,0:T(8,128)(2,1)S(1)}, bf16[512,768]{1,0:T(8,128)(2,1)}) custom-call(bf16[512,768]{1,0:T(8,128)(2,1)S(1)} %copy-done, bf16[512,768]{1,0:T(8,128)(2,1)S(1)} %copy-done.2, bf16[768,768]{1,0:T(8,128)(2,1)} %get-tuple-element.87.refs_2_, bf16[768,768]{1,0:T(8,128)(2,1)} %collective-permute-done.1.refs_3_, ...), custom_call_target="tpu_custom_call" | custom-call | flops 100000000 | tf_op jit(solution)/shard_map/pallas_call | solution.py:49
  152.5 6.5 %collective-permute-done.27 = bf16[96,768]{1,0:T(8,128)(2,1)S(1)} collective-permute-done((bf16[96,768]{1,0:T(8,128)(2,1)S(1)}, bf16[96,768]{1,0:T(8,128)(2,1)S(1)}, u32[]{:S(2)}, u32[]{:S(2)}) %collective-permute-start.27) | collective-permute-done | bytes 147488 | tf_op jit(solution)/shard_map/ppermute | solution.py:436
  161.9 6.3 %collective-permute-done.28 = bf16[96,768]{1,0:T(8,128)(2,1)S(1)} collective-permute-done((bf16[96,768]{1,0:T(8,128)(2,1)S(1)}, bf16[96,768]{1,0:T(8,128)(2,1)S(1)}, u32[]{:S(2)}, u32[]{:S(2)}) %collective-permute-start.28) | collective-permute-done | bytes 147488 | tf_op jit(solution)/shard_map/ppermute | solution.py:436
  178.1 4.7 %collective-permute-done.35 = bf16[96,768]{1,0:T(8,128)(2,1)S(1)} collective-permute-done((bf16[96,768]{1,0:T(8,128)(2,1)S(1)}, bf16[96,768]{1,0:T(8,128)(2,1)S(1)}, u32[]{:S(2)}, u32[]{:S(2)}) %collective-permute-start.35) | collective-permute-done | bytes 147488 | tf_op jit(solution)/shard_map/ppermute | solution.py:436
  184.2 3.2 %collective-permute-done.33 = bf16[192,768]{1,0:T(8,128)(2,1)} collective-permute-done((bf16[192,768]{1,0:T(8,128)(2,1)S(1)}, bf16[192,768]{1,0:T(8,128)(2,1)}, u32[]{:S(2)}, u32[]{:S(2)}) %collective-permute-start.33) | collective-permute-done | bytes 294944 | tf_op jit(solution)/shard_map/ppermute | solution.py:436
  196.2 8.8 %collective-permute-done.41 = bf16[192,768]{1,0:T(8,128)(2,1)S(1)} collective-permute-done((bf16[192,768]{1,0:T(8,128)(2,1)S(1)}, bf16[192,768]{1,0:T(8,128)(2,1)S(1)}, u32[]{:S(2)}, u32[]{:S(2)}) %collective-permute-start.41) | collective-permute-done | bytes 294944 | tf_op jit(solution)/shard_map/ppermute | solution.py:436
  207.3 8.9 %collective-permute-done.38 = bf16[100,768]{1,0:T(8,128)(2,1)S(1)} collective-permute-done((bf16[100,768]{1,0:T(8,128)(2,1)S(1)}, bf16[100,768]{1,0:T(8,128)(2,1)S(1)}, u32[]{:S(2)}, u32[]{:S(2)}) %collective-permute-start.38) | collective-permute-done | bytes 153632 | tf_op jit(solution)/shard_map/ppermute | solution.py:436
  216.4 7.0 %collective-permute-done.40 = bf16[100,768]{1,0:T(8,128)(2,1)S(1)} collective-permute-done((bf16[100,768]{1,0:T(8,128)(2,1)S(1)}, bf16[100,768]{1,0:T(8,128)(2,1)S(1)}, u32[]{:S(2)}, u32[]{:S(2)}) %collective-permute-start.40) | collective-permute-done | bytes 153632 | tf_op jit(solution)/shard_map/ppermute | solution.py:436
  224.0 6.4 %collective-permute-done.42 = bf16[200,768]{1,0:T(8,128)(2,1)S(1)} collective-permute-done((bf16[200,768]{1,0:T(8,128)(2,1)S(1)}, bf16[200,768]{1,0:T(8,128)(2,1)S(1)}, u32[]{:S(2)}, u32[]{:S(2)}) %collective-permute-start.42) | collective-permute-done | bytes 307232 | tf_op jit(solution)/shard_map/ppermute | solution.py:436
  235.3 5.6 %collective-permute-done.44 = bf16[400,768]{1,0:T(8,128)(2,1)S(1)} collective-permute-done((bf16[400,768]{1,0:T(8,128)(2,1)S(1)}, bf16[400,768]{1,0:T(8,128)(2,1)S(1)}, u32[]{:S(2)}, u32[]{:S(2)}) %collective-permute-start.44) | collective-permute-done | bytes 614432 | tf_op jit(solution)/shard_map/ppermute | solution.py:436
  (204 shorter events, 94.6 us)
Async XLA Ops:
  11.6 16.4 %collective-permute-start = (bf16[384,768]{1,0:T(8,128)(2,1)}, bf16[384,768]{1,0:T(8,128)(2,1)S(1)}, u32[]{:S(2)}, u32[]{:S(2)}) collective-permute-start(bf16[384,768]{1,0:T(8,128)(2,1)} %get-tuple-element.86), channel_id=1, source_target_pairs={{0,2},{1,3},{2,0},{3,1},{4,6},{5,7},{6,4},{7,5},{8,10},{9,11},{10,... | collective-permute-start | bytes 1769480 | tf_op jit(solution)/shard_map/ppermute | solution.py:436
  11.7 27.7 %collective-permute-start.8 = (bf16[384,768]{1,0:T(8,128)(2,1)S(1)}, bf16[384,768]{1,0:T(8,128)(2,1)S(1)}, u32[]{:S(2)}, u32[]{:S(2)}) collective-permute-start(bf16[384,768]{1,0:T(8,128)(2,1)S(1)} %constant_dynamic-slice_fusion.10), channel_id=1, source_target_pairs={{0,2},{1,3},{2,0},{3,1},{4,6},{5,7},{6,4},{7,5},{8,10},{9,11},{10,... | collective-permute-start | bytes 1769480 | tf_op jit(solution)/shard_map/ppermute | solution.py:436
  28.1 14.1 %collective-permute-start.4 = (bf16[384,768]{1,0:T(8,128)(2,1)S(1)}, bf16[384,768]{1,0:T(8,128)(2,1)S(1)}, u32[]{:S(2)}, u32[]{:S(2)}) collective-permute-start(bf16[384,768]{1,0:T(8,128)(2,1)S(1)} %collective-permute-done.refs_2_.refs_3_), channel_id=1, source_target_pairs={{0,4},{4,0},{8,12},{12,8},{16,20},{20,16},{24,28},{28,24},{1,5},{5... | collective-permute-start | bytes 1769480 | tf_op jit(solution)/shard_map/ppermute | solution.py:436
  29.6 12.6 %collective-permute-start.5 = (bf16[384,768]{1,0:T(8,128)(2,1)S(1)}, bf16[384,768]{1,0:T(8,128)(2,1)S(1)}, u32[]{:S(2)}, u32[]{:S(2)}) collective-permute-start(bf16[384,768]{1,0:T(8,128)(2,1)S(1)} %collective-permute-done.refs_2_.refs_3_), channel_id=1, source_target_pairs={{0,1},{1,0},{2,3},{3,2},{4,5},{5,4},{6,7},{7,6},{8,9},{9,8},{10,11... | collective-permute-start | bytes 1769480 | tf_op jit(solution)/shard_map/ppermute | solution.py:436
  29.6 29.0 %collective-permute-start.15 = (bf16[768,768]{1,0:T(8,128)(2,1)S(1)}, bf16[768,768]{1,0:T(8,128)(2,1)S(1)}, u32[]{:S(2)}, u32[]{:S(2)}) collective-permute-start(bf16[768,768]{1,0:T(8,128)(2,1)S(1)} %copy-done.3), channel_id=1, source_target_pairs={{0,1},{1,0},{2,3},{3,2},{4,5},{5,4},{6,7},{7,6},{8,9},{9,8},{10,11... | collective-permute-start | bytes 3538952 | tf_op jit(solution)/shard_map/ppermute | solution.py:436
  30.1 28.5 %collective-permute-start.16 = (bf16[768,768]{1,0:T(8,128)(2,1)S(1)}, bf16[768,768]{1,0:T(8,128)(2,1)S(1)}, u32[]{:S(2)}, u32[]{:S(2)}) collective-permute-start(bf16[768,768]{1,0:T(8,128)(2,1)S(1)} %copy-done.4), channel_id=1, source_target_pairs={{0,1},{1,0},{2,3},{3,2},{4,5},{5,4},{6,7},{7,6},{8,9},{9,8},{10,11... | collective-permute-start | bytes 3538952 | tf_op jit(solution)/shard_map/ppermute | solution.py:436
  40.7 15.4 %collective-permute-start.9 = (bf16[384,768]{1,0:T(8,128)(2,1)S(1)}, bf16[384,768]{1,0:T(8,128)(2,1)S(1)}, u32[]{:S(2)}, u32[]{:S(2)}) collective-permute-start(bf16[384,768]{1,0:T(8,128)(2,1)S(1)} %collective-permute-done.8.refs_2_.refs_8_), channel_id=1, source_target_pairs={{0,4},{4,0},{8,12},{12,8},{16,20},{20,16},{24,28},{28,24},{1,5},{5... | collective-permute-start | bytes 1769480 | tf_op jit(solution)/shard_map/ppermute | solution.py:436
  42.2 15.8 %collective-permute-start.12 = (bf16[384,768]{1,0:T(8,128)(2,1)S(1)}, bf16[384,768]{1,0:T(8,128)(2,1)S(1)}, u32[]{:S(2)}, u32[]{:S(2)}) collective-permute-start(bf16[384,768]{1,0:T(8,128)(2,1)S(1)} %constant_dynamic-slice_fusion.9), channel_id=1, source_target_pairs={{0,2},{1,3},{2,0},{3,1},{4,6},{5,7},{6,4},{7,5},{8,10},{9,11},{10,... | collective-permute-start | bytes 1769480 | tf_op jit(solution)/shard_map/ppermute | solution.py:436
  44.2 17.6 %collective-permute-start.10 = (bf16[384,768]{1,0:T(8,128)(2,1)S(1)}, bf16[384,768]{1,0:T(8,128)(2,1)S(1)}, u32[]{:S(2)}, u32[]{:S(2)}) collective-permute-start(bf16[384,768]{1,0:T(8,128)(2,1)S(1)} %collective-permute-done.8.refs_2_.refs_8_), channel_id=1, source_target_pairs={{0,1},{1,0},{2,3},{3,2},{4,5},{5,4},{6,7},{7,6},{8,9},{9,8},{10,11... | collective-permute-start | bytes 1769480 | tf_op jit(solution)/shard_map/ppermute | solution.py:436
  58.0 15.0 %collective-permute-start.13 = (bf16[384,768]{1,0:T(8,128)(2,1)S(1)}, bf16[384,768]{1,0:T(8,128)(2,1)S(1)}, u32[]{:S(2)}, u32[]{:S(2)}) collective-permute-start(bf16[384,768]{1,0:T(8,128)(2,1)S(1)} %collective-permute-done.12.refs_2_.refs_4_), channel_id=1, source_target_pairs={{0,4},{4,0},{8,12},{12,8},{16,20},{20,16},{24,28},{28,24},{1,5},{5... | collective-permute-start | bytes 1769480 | tf_op jit(solution)/shard_map/ppermute | solution.py:436
  58.5 14.4 %collective-permute-start.14 = (bf16[384,768]{1,0:T(8,128)(2,1)S(1)}, bf16[384,768]{1,0:T(8,128)(2,1)S(1)}, u32[]{:S(2)}, u32[]{:S(2)}) collective-permute-start(bf16[384,768]{1,0:T(8,128)(2,1)S(1)} %collective-permute-done.12.refs_2_.refs_4_), channel_id=1, source_target_pairs={{0,1},{1,0},{2,3},{3,2},{4,5},{5,4},{6,7},{7,6},{8,9},{9,8},{10,11... | collective-permute-start | bytes 1769480 | tf_op jit(solution)/shard_map/ppermute | solution.py:436
  89.0 29.0 %collective-permute-start.21 = (bf16[768,768]{1,0:T(8,128)(2,1)S(1)}, bf16[768,768]{1,0:T(8,128)(2,1)}, u32[]{:S(2)}, u32[]{:S(2)}) collective-permute-start(bf16[768,768]{1,0:T(8,128)(2,1)S(1)} %reduce-precision_convert_fusion.8.refs_12_), channel_id=1, source_target_pairs={{0,2},{1,3},{2,0},{3,1},{4,6},{5,7},{6,4},{7,5},{8,10},{9,11},{10,... | collective-permute-start | bytes 3538952 | tf_op jit(solution)/shard_map/ppermute | solution.py:436
  90.0 28.1 %collective-permute-start.20 = (bf16[768,768]{1,0:T(8,128)(2,1)}, bf16[768,768]{1,0:T(8,128)(2,1)}, u32[]{:S(2)}, u32[]{:S(2)}) collective-permute-start(bf16[768,768]{1,0:T(8,128)(2,1)} %get-tuple-element.132), channel_id=1, source_target_pairs={{0,1},{1,0},{2,3},{3,2},{4,5},{5,4},{6,7},{7,6},{8,9},{9,8},{10,11... | collective-permute-start | bytes 3538952 | tf_op jit(solution)/shard_map/ppermute | solution.py:436
  108.6 13.4 %collective-permute-start.22 = (bf16[800,768]{1,0:T(8,128)(2,1)}, bf16[800,768]{1,0:T(8,128)(2,1)}, u32[]{:S(2)}, u32[]{:S(2)}) collective-permute-start(bf16[800,768]{1,0:T(8,128)(2,1)} %get-tuple-element.135), channel_id=1, source_target_pairs={{0,1},{1,0},{2,3},{3,2},{4,5},{5,4},{6,7},{7,6},{8,9},{9,8},{10,11... | collective-permute-start | bytes 3686408 | tf_op jit(solution)/shard_map/ppermute | solution.py:436
  109.1 34.2 %collective-permute-start.30 = (bf16[768,768]{1,0:T(8,128)(2,1)}, bf16[768,768]{1,0:T(8,128)(2,1)}, u32[]{:S(2)}, u32[]{:S(2)}) collective-permute-start(bf16[768,768]{1,0:T(8,128)(2,1)} %reduce-precision_convert_fusion.7.refs_15_), channel_id=1, source_target_pairs={{0,2},{1,3},{2,0},{3,1},{4,6},{5,7},{6,4},{7,5},{8,10},{9,11},{10,... | collective-permute-start | bytes 3538952 | tf_op jit(solution)/shard_map/ppermute | solution.py:436
  110.2 33.1 %collective-permute-start.29 = (bf16[768,768]{1,0:T(8,128)(2,1)}, bf16[768,768]{1,0:T(8,128)(2,1)}, u32[]{:S(2)}, u32[]{:S(2)}) collective-permute-start(bf16[768,768]{1,0:T(8,128)(2,1)} %copy-done.24), channel_id=1, source_target_pairs={{0,1},{1,0},{2,3},{3,2},{4,5},{5,4},{6,7},{7,6},{8,9},{9,8},{10,11... | collective-permute-start | bytes 3538952 | tf_op jit(solution)/shard_map/ppermute | solution.py:436
  121.4 17.6 %collective-permute-start.25 = (bf16[384,768]{1,0:T(8,128)(2,1)}, bf16[384,768]{1,0:T(8,128)(2,1)}, u32[]{:S(2)}, u32[]{:S(2)}) collective-permute-start(bf16[384,768]{1,0:T(8,128)(2,1)} %constant_dynamic-slice_fusion.8), channel_id=1, source_target_pairs={{0,4},{4,0},{8,12},{12,8},{16,20},{20,16},{24,28},{28,24},{1,5},{5... | collective-permute-start | bytes 1769480 | tf_op jit(solution)/shard_map/ppermute | solution.py:436
  124.0 44.8 %collective-permute-start.24 = (bf16[800,768]{1,0:T(8,128)(2,1)S(1)}, bf16[800,768]{1,0:T(8,128)(2,1)}, u32[]{:S(2)}, u32[]{:S(2)}) collective-permute-start(bf16[800,768]{1,0:T(8,128)(2,1)S(1)} %reduce-precision_convert_fusion.2.refs_15_), channel_id=1, source_target_pairs={{0,2},{1,3},{2,0},{3,1},{4,6},{5,7},{6,4},{7,5},{8,10},{9,11},{10,... | collective-permute-start | bytes 3686408 | tf_op jit(solution)/shard_map/ppermute | solution.py:436
  138.9 29.9 %collective-permute-start.23 = (bf16[800,768]{1,0:T(8,128)(2,1)}, bf16[800,768]{1,0:T(8,128)(2,1)}, u32[]{:S(2)}, u32[]{:S(2)}) collective-permute-start(bf16[800,768]{1,0:T(8,128)(2,1)} %get-tuple-element.138), channel_id=1, source_target_pairs={{0,1},{1,0},{2,3},{3,2},{4,5},{5,4},{6,7},{7,6},{8,9},{9,8},{10,11... | collective-permute-start | bytes 3686408 | tf_op jit(solution)/shard_map/ppermute | solution.py:436
  146.4 14.3 %collective-permute-start.31 = (bf16[384,768]{1,0:T(8,128)(2,1)}, bf16[384,768]{1,0:T(8,128)(2,1)}, u32[]{:S(2)}, u32[]{:S(2)}) collective-permute-start(bf16[384,768]{1,0:T(8,128)(2,1)} %constant_dynamic-slice_fusion.5), channel_id=1, source_target_pairs={{0,4},{4,0},{8,12},{12,8},{16,20},{20,16},{24,28},{28,24},{1,5},{5... | collective-permute-start | bytes 1769480 | tf_op jit(solution)/shard_map/ppermute | solution.py:436
  171.1 20.0 %collective-permute-start.32 = (bf16[400,768]{1,0:T(8,128)(2,1)S(1)}, bf16[400,768]{1,0:T(8,128)(2,1)S(1)}, u32[]{:S(2)}, u32[]{:S(2)}) collective-permute-start(bf16[400,768]{1,0:T(8,128)(2,1)S(1)} %constant_dynamic-slice_fusion.4), channel_id=1, source_target_pairs={{0,4},{4,0},{8,12},{12,8},{16,20},{20,16},{24,28},{28,24},{1,5},{5... | collective-permute-start | bytes 1843208 | tf_op jit(solution)/shard_map/ppermute | solution.py:436
  191.5 13.4 %collective-permute-start.36 = (bf16[200,768]{1,0:T(8,128)(2,1)S(1)}, bf16[200,768]{1,0:T(8,128)(2,1)S(1)}, u32[]{:S(2)}, u32[]{:S(2)}) collective-permute-start(bf16[200,768]{1,0:T(8,128)(2,1)S(1)} %constant_dynamic-slice_fusion.1), channel_id=1, source_target_pairs={{0,8},{4,12},{8,0},{12,4},{16,24},{20,28},{24,16},{28,20},{1,9},{5... | collective-permute-start | bytes 921608 | tf_op jit(solution)/shard_map/ppermute | solution.py:436
  192.6 12.3 %collective-permute-start.41 = (bf16[192,768]{1,0:T(8,128)(2,1)S(1)}, bf16[192,768]{1,0:T(8,128)(2,1)S(1)}, u32[]{:S(2)}, u32[]{:S(2)}) collective-permute-start(bf16[192,768]{1,0:T(8,128)(2,1)S(1)} %maximum_select_fusion.8), channel_id=1, source_target_pairs={{0,8},{4,12},{8,0},{12,4},{16,24},{20,28},{24,16},{28,20},{1,9},{5... | collective-permute-start | bytes 884744 | tf_op jit(solution)/shard_map/ppermute | solution.py:436
  205.3 18.2 %collective-permute-start.43 = (bf16[384,768]{1,0:T(8,128)(2,1)S(1)}, bf16[384,768]{1,0:T(8,128)(2,1)S(1)}, u32[]{:S(2)}, u32[]{:S(2)}) collective-permute-start(bf16[384,768]{1,0:T(8,128)(2,1)S(1)} %maximum_select_fusion.5), channel_id=1, source_target_pairs={{0,4},{4,0},{8,12},{12,8},{16,20},{20,16},{24,28},{28,24},{1,5},{5... | collective-permute-start | bytes 1769480 | tf_op jit(solution)/shard_map/ppermute | solution.py:436
  (57 other events, 304.5 us)
